TPU v7x, 512 devices: a whole 4x4x16 slice. The times are simulated.
512 devices in a mesh: lon: 32 (over z, x_hi), chan: 16 (over x_lo, y, core).
Axes of the slice: x: 4 (x_hi: 2, x_lo: 2; x = x_hi * 2 + x_lo), y: 4, z: 16, core: 2. Of those that a mesh axis runs over, the one named last changes fastest.
Arguments:
- features: bfloat16 [48, 256, 2048], P(None, 'lon', 'chan'), may hold values from -6 to 6
- w_point: bfloat16 [2048, 256], P('chan'), may hold values from -0.125 to 0.125
- w_dilated: bfloat16 [3, 3, 3, 2048, 256], P(None, None, None, 'chan'), may hold values from -0.046875 to 0.046875
- w_pool: bfloat16 [2048, 256], P('chan'), may hold values from -0.125 to 0.125
- bn_scale: float32 [5, 256], replicated, may hold values from 0.25 to 1.75
- bn_shift: float32 [5, 256], replicated, may hold values from -3 to 3
- proj_weight: bfloat16 [5, 256, 256], P(None, None, 'chan'), may hold values from -0.15625 to 0.15625
- proj_scale: float32 [256], P('chan'), may hold values from 0.25 to 1.75
- proj_shift: float32 [256], P('chan'), may hold values from -3 to 3
- skip: bfloat16 [48, 256, 48], P(None, 'lon'), may hold values from -6 to 6
- merge_weight: bfloat16 [3, 3, 304, 256], P(None, None, None, 'chan'), may hold values from -0.109375 to 0.109375
- merge_scale: float32 [256], P('chan'), may hold values from 0.25 to 1.75
- merge_shift: float32 [256], P('chan'), may hold values from -3 to 3
Outputs:
- merged: bfloat16 [48, 256, 256], P(None, 'lon', 'chan')
All inputs are finite; a program needn't handle non-finite values.
Results may differ from a plain program's by a relative error of at most 0.0065.
Values may be sent and summed in bfloat16 or wider, within the bound.
A program may use at most 64 MiB of HBM per device.

v0:
```python
import jax
import jax.numpy as jnp
from jax import lax
from jax.sharding import PartitionSpec as P

dilations = (12, 24, 36)


def shifted(value, axis, steps):
    count = lax.axis_size(axis)
    pairs = [(source, (source + steps) % count) for source in range(count)]
    return lax.ppermute(value, axis, pairs)


def extended(array, sides, width):
    for axis, dim in sides:
        devices, length = (lax.axis_size(axis), array.shape[dim])
        up = [(i, (i + 1) % devices) for i in range(devices)]
        down = [(j, i) for i, j in up]
        last = lax.slice_in_dim(array, length - width, length, axis=dim)
        leading = lax.slice_in_dim(array, 0, width, axis=dim)
        before = lax.ppermute(last, axis, up)
        after = lax.ppermute(leading, axis, down)
        array = jnp.concatenate([before, array, after], axis=dim)
    return array


def tap_sum(padded, weights, dilation, margin, out_rows, out_cols):
    running = jnp.zeros((out_rows * out_cols, weights.shape[-1]), jnp.float32)
    for tap_row in range(3):
        for tap_col in range(3):
            top = margin + (tap_row - 1) * dilation
            left = margin + (tap_col - 1) * dilation
            window = padded[top : top + out_rows, left : left + out_cols]
            running = running + jnp.dot(
                window.reshape(out_rows * out_cols, -1),
                weights[tap_row, tap_col],
                preferred_element_type=jnp.float32,
            )
    return running


def body(
    features,
    w_point,
    w_dilated,
    w_pool,
    bn_scale,
    bn_shift,
    proj_weight,
    proj_scale,
    proj_shift,
    skip,
    merge_weight,
    merge_scale,
    merge_shift,
):
    cell_rows, cell_cols, chan_local = features.shape
    cell_count = cell_rows * cell_cols
    rim_width = max(dilations)
    flat = features.reshape(cell_count, chan_local)
    channel_sums = jnp.sum(flat, axis=0, dtype=jnp.float32).reshape(1, chan_local)
    image_part = jnp.dot(channel_sums, w_pool.astype(jnp.float32), precision=lax.Precision.HIGHEST)
    image_total = lax.psum(image_part, ("lon", "chan"))
    image = image_total / (cell_count * lax.axis_size("lon"))
    hop_total = -(-rim_width // cell_cols)
    west_parts = []
    east_parts = []
    for hop_index in range(1, hop_total + 1):
        span_cols = min(cell_cols, rim_width - (hop_index - 1) * cell_cols)
        west_parts.insert(0, shifted(features[:, cell_cols - span_cols :], "lon", hop_index))
        east_parts.append(shifted(features[:, :span_cols], "lon", -hop_index))
    point_out = jnp.dot(flat, w_point, preferred_element_type=jnp.float32)
    wrapped = jnp.concatenate(west_parts + [features] + east_parts, axis=1)
    padded = jnp.pad(wrapped, ((rim_width, rim_width), (0, 0), (0, 0)))
    outputs = [point_out]
    for rate_index, dilation in enumerate(dilations):
        outputs.append(
            tap_sum(padded, w_dilated[rate_index], dilation, rim_width, cell_rows, cell_cols)
        )
    partial_sums = jnp.stack(outputs, axis=1)
    branch_width = partial_sums.shape[2]
    summed = lax.psum(partial_sums, "chan")
    image_field = jnp.broadcast_to(image.reshape(1, 1, branch_width), (cell_count, 1, branch_width))
    branches = jnp.concatenate([summed, image_field], axis=1)
    activated = jax.nn.relu(branches * bn_scale + bn_shift).astype(jnp.bfloat16)
    out_local = proj_weight.shape[2]
    projected = jnp.dot(
        activated.reshape(cell_count, 5 * branch_width),
        proj_weight.reshape(5 * branch_width, out_local),
        preferred_element_type=jnp.float32,
    )
    pooled_own = (
        jax.nn.relu(projected * proj_scale + proj_shift)
        .astype(jnp.bfloat16)
        .reshape(cell_rows, cell_cols, out_local)
    )
    pooled = lax.all_gather(pooled_own, "chan", axis=2, tiled=True)
    joined = jnp.concatenate([pooled, skip], axis=2)
    bordered = extended(joined, (("lon", 1),), 1)
    bordered = jnp.pad(bordered, ((1, 1), (0, 0), (0, 0)))
    mixed = tap_sum(bordered, merge_weight, 1, 1, cell_rows, cell_cols)
    return (
        jax.nn.relu(mixed * merge_scale + merge_shift)
        .astype(jnp.bfloat16)
        .reshape(cell_rows, cell_cols, out_local)
    )


def solution(mesh):
    return jax.shard_map(
        body,
        mesh=mesh,
        in_specs=(
            P(None, "lon", "chan"),
            P("chan", None),
            P(None, None, None, "chan", None),
            P("chan", None),
            P(),
            P(),
            P(None, None, "chan"),
            P("chan"),
            P("chan"),
            P(None, "lon", None),
            P(None, None, None, "chan"),
            P("chan"),
            P("chan"),
        ),
        out_specs=P(None, "lon", "chan"),
        check_vma=False,
    )
```

profile of v0, /device:TPU:1, one launch (start us, length us, event | category | flops | bytes accessed | tf_op | source)
XLA Modules:
  0.0 271.1 jit_solution(15135609458156420169)
XLA Ops:
  6.5 5.9 %collective-permute-start.1 = (bf16[48,8,128]{2,1,0:T(8,128)(2,1)}, bf16[48,8,128]{2,1,0:T(8,128)(2,1)S(1)}, u32[]{:S(2)}, u32[]{:S(2)}) collective-permute-start(bf16[48,8,128]{2,1,0:T(8,128)(2,1)} %param.13), channel_id=1, source_target_pairs={{0,64},{16,80},{32,96},{48,112},{64,128},{80,144},{96,160},{112,17... | collective-permute-start | bytes 294920 | tf_op jit(solution)/shard_map/ppermute | solution.py:12
  12.4 6.0 %collective-permute-start.2 = (bf16[48,8,128]{2,1,0:T(8,128)(2,1)}, bf16[48,8,128]{2,1,0:T(8,128)(2,1)S(1)}, u32[]{:S(2)}, u32[]{:S(2)}) collective-permute-start(bf16[48,8,128]{2,1,0:T(8,128)(2,1)} %param.13), channel_id=1, source_target_pairs={{0,48},{16,64},{32,80},{48,96},{64,112},{80,128},{96,144},{112,160... | collective-permute-start | bytes 294920 | tf_op jit(solution)/shard_map/ppermute | solution.py:12
  18.4 4.8 %collective-permute-start.3 = (bf16[48,8,128]{2,1,0:T(8,128)(2,1)}, bf16[48,8,128]{2,1,0:T(8,128)(2,1)S(1)}, u32[]{:S(2)}, u32[]{:S(2)}) collective-permute-start(bf16[48,8,128]{2,1,0:T(8,128)(2,1)} %param.13), channel_id=1, source_target_pairs={{0,32},{16,48},{32,64},{48,80},{64,96},{80,112},{96,128},{112,144}... | collective-permute-start | bytes 294920 | tf_op jit(solution)/shard_map/ppermute | solution.py:12
  23.2 1.0 fusion.179
  24.2 6.2 %collective-permute-start = (bf16[48,4,128]{2,1,0:T(4,128)(2,1)S(1)}, bf16[48,4,128]{2,1,0:T(4,128)(2,1)S(1)}, u32[]{:S(2)}, u32[]{:S(2)}) collective-permute-start(bf16[48,4,128]{2,1,0:T(4,128)(2,1)S(1)} %get-tuple-element.19), channel_id=1, source_target_pairs={{0,80},{16,96},{32,112},{48,128},{64,144},{80,160},{96,176},{112,1... | collective-permute-start | bytes 147464 | tf_op jit(solution)/shard_map/ppermute | solution.py:12
  30.4 4.6 %collective-permute-start.9 = (bf16[48,4,128]{2,1,0:T(4,128)(2,1)S(1)}, bf16[48,4,128]{2,1,0:T(4,128)(2,1)}, u32[]{:S(2)}, u32[]{:S(2)}) collective-permute-start(bf16[48,4,128]{2,1,0:T(4,128)(2,1)S(1)} %get-tuple-element.18), channel_id=1, source_target_pairs={{0,432},{16,448},{32,464},{48,480},{64,496},{80,0},{96,16},{112,32... | collective-permute-start | bytes 147464 | tf_op jit(solution)/shard_map/ppermute | solution.py:12
  35.1 1.5 slice_bitcast_fusion.2
  36.6 1.0 fusion.131
  37.6 0.9 fusion.129
  38.5 1.0 fusion.127
  39.5 2.6 collective-permute-start.4
  42.1 6.3 %collective-permute-start.5 = (bf16[48,8,128]{2,1,0:T(8,128)(2,1)S(1)}, bf16[48,8,128]{2,1,0:T(8,128)(2,1)S(1)}, u32[]{:S(2)}, u32[]{:S(2)}) collective-permute-start(bf16[48,8,128]{2,1,0:T(8,128)(2,1)S(1)} %copy-done.1), channel_id=1, source_target_pairs={{0,496},{16,0},{32,16},{48,32},{64,48},{80,64},{96,80},{112,96},{1... | collective-permute-start | bytes 294920 | tf_op jit(solution)/shard_map/ppermute | solution.py:12
  48.4 1.9 collective-permute-start.6
  50.4 3.9 %collective-permute-start.7 = (bf16[48,8,128]{2,1,0:T(8,128)(2,1)S(1)}, bf16[48,8,128]{2,1,0:T(8,128)(2,1)S(1)}, u32[]{:S(2)}, u32[]{:S(2)}) collective-permute-start(bf16[48,8,128]{2,1,0:T(8,128)(2,1)S(1)} %copy-done.1), channel_id=1, source_target_pairs={{0,464},{16,480},{32,496},{48,0},{64,16},{80,32},{96,48},{112,64},... | collective-permute-start | bytes 294920 | tf_op jit(solution)/shard_map/ppermute | solution.py:12
  54.3 5.2 %collective-permute-start.8 = (bf16[48,8,128]{2,1,0:T(8,128)(2,1)S(1)}, bf16[48,8,128]{2,1,0:T(8,128)(2,1)S(1)}, u32[]{:S(2)}, u32[]{:S(2)}) collective-permute-start(bf16[48,8,128]{2,1,0:T(8,128)(2,1)S(1)} %copy-done.1), channel_id=1, source_target_pairs={{0,448},{16,464},{32,480},{48,496},{64,0},{80,16},{96,32},{112,48}... | collective-permute-start | bytes 294920 | tf_op jit(solution)/shard_map/ppermute | solution.py:12
  59.8 0.6 copy-done.13
  60.4 0.6 copy-done.7
  61.0 3.8 %collective-permute-done.8 = bf16[48,8,128]{2,1,0:T(8,128)(2,1)S(1)} collective-permute-done((bf16[48,8,128]{2,1,0:T(8,128)(2,1)S(1)}, bf16[48,8,128]{2,1,0:T(8,128)(2,1)S(1)}, u32[]{:S(2)}, u32[]{:S(2)}) %collective-permute-start.8) | collective-permute-done | bytes 98336 | tf_op jit(solution)/shard_map/ppermute | solution.py:12
  64.8 13.3 %concatenate.30 = bf16[48,80,128]{2,1,0:T(8,128)(2,1)S(1)} concatenate(bf16[48,4,128]{2,1,0:T(4,128)(2,1)S(1)} %collective-permute-done, bf16[48,8,128]{2,1,0:T(8,128)(2,1)} %copy-done.9, bf16[48,8,128]{2,1,0:T(8,128)(2,1)} %copy-done.15, bf16[48,8,128]{2,1,0:T(8,128)(2,1)} %copy-done.11, bf16[48,8,128]{2,1,0:T(8,128)(2,1)} %copy-done.13, bf16[48,8,128]{2,1,0:T(8,128)(2,1)S(1)} %copy-done.1, ...), dimensions={1} | concatenate | bytes 1966080 | tf_op jit(solution)/shard_map/concatenate | solution.py:74
  81.1 0.5 copy-done.12
  81.8 0.2 fusion.23
  82.1 0.5 copy-done.16
  83.1 0.4 copy-done.10
  84.1 0.3 copy-done.6
  84.4 0.2 fusion.21
  84.6 0.7 copy-done.8
  85.5 1.0 fusion.11
  86.5 1.3 pad_maximum_fusion
  88.2 103.9 %psum.15 = f32[1,256]{1,0:T(1,128)S(1)} all-reduce(f32[1,256]{1,0:T(1,128)S(1)} %fusion.152), channel_id=1, replica_groups=mesh['lon'=32,'chan'=16] {'lon','chan'}, use_global_device_ids=true, to_apply=%region_2.3 | all-reduce | flops 256 | bytes 2048 | tf_op jit(solution)/shard_map/psum | solution.py:64
  192.0 31.6 %all-reduce.4.cloned.1.call-done = f32[384,4,256]{2,0,1:T(8,128)} async-done(((f32[384,4,256]{2,0,1:T(8,128)}), f32[384,4,256]{2,0,1:T(8,128)}) %all-reduce.4.cloned.1.call-update) | async-done | bytes 1572880 | tf_op jit(solution)/shard_map/psum | solution.py:83
  223.7 1.8 fusion.30
  225.8 19.0 %all_gather.3 = bf16[48,8,256]{0,1,2:T(8,128)(2,1)S(1)} all-gather(bf16[48,8,16]{0,1,2:T(8,128)(2,1)S(1)} %copy.54), channel_id=1, replica_groups=mesh['lon'=32,'chan'=16] {'chan'}, dimensions={2}, use_global_device_ids=true | all-gather | bytes 208896 | tf_op jit(solution)/shard_map/all_gather | solution.py:98
  244.8 0.4 fusion.57
  245.2 3.7 %collective-permute-start.10 = (bf16[48,1,304]{0,1,2:T(2,128)(2,1)S(1)}, bf16[48,1,304]{0,1,2:T(2,128)(2,1)S(1)}, u32[]{:S(2)}, u32[]{:S(2)}) collective-permute-start(bf16[48,1,304]{0,1,2:T(2,128)(2,1)S(1)} %get-tuple-element.8), channel_id=1, source_target_pairs={{0,16},{16,32},{32,48},{48,64},{64,80},{80,96},{96,112},{112,128},... | collective-permute-start | bytes 87560 | tf_op jit(solution)/shard_map/ppermute | solution.py:22
  248.9 5.4 %collective-permute-start.11 = (bf16[48,1,304]{0,1,2:T(2,128)(2,1)S(1)}, bf16[48,1,304]{0,1,2:T(2,128)(2,1)S(1)}, u32[]{:S(2)}, u32[]{:S(2)}) collective-permute-start(bf16[48,1,304]{0,1,2:T(2,128)(2,1)S(1)} %get-tuple-element.9), channel_id=1, source_target_pairs={{16,0},{32,16},{48,32},{64,48},{80,64},{96,80},{112,96},{128,112},... | collective-permute-start | bytes 87560 | tf_op jit(solution)/shard_map/ppermute | solution.py:23
  254.4 0.4 copy.57
  254.8 0.5 copy.65
  255.3 1.1 collective-permute-done.10
  256.6 3.6 %collective-permute-done.11 = bf16[48,1,304]{0,1,2:T(2,128)(2,1)S(1)} collective-permute-done((bf16[48,1,304]{0,1,2:T(2,128)(2,1)S(1)}, bf16[48,1,304]{0,1,2:T(2,128)(2,1)S(1)}, u32[]{:S(2)}, u32[]{:S(2)}) %collective-permute-start.11) | collective-permute-done | bytes 29216 | tf_op jit(solution)/shard_map/ppermute | solution.py:23
  260.7 0.7 copy-done.19
  261.8 0.2 convolution_add_fusion.12
  262.0 0.2 convolution_add_fusion.11
  262.2 0.2 convolution_add_fusion.10
  262.5 0.2 convolution_add_fusion.9
  262.7 0.2 convolution_add_fusion.8
  262.9 0.2 convolution_add_fusion.7
  263.2 0.2 fusion.31
  263.6 0.7 copy.73
  (95 shorter events, 6.7 us)
Async XLA Ops:
  6.5 53.0 %copy-start = (bf16[128,256]{1,0:T(8,128)(2,1)S(1)}, bf16[128,256]{1,0:T(8,128)(2,1)}, u32[]{:S(2)}) copy-start(bf16[128,256]{1,0:T(8,128)(2,1)} %param.14) | copy-start | bytes 196612
  6.5 217.1 %all-reduce.4.cloned.1.call-start = ((), (), s32[]{:S(2)}) async-start(), calls=%async_computation | async-start | bytes 3145728 | tf_op jit(solution)/shard_map/psum | solution.py:83
  6.5 41.8 %collective-permute-start.1 = (bf16[48,8,128]{2,1,0:T(8,128)(2,1)}, bf16[48,8,128]{2,1,0:T(8,128)(2,1)S(1)}, u32[]{:S(2)}, u32[]{:S(2)}) collective-permute-start(bf16[48,8,128]{2,1,0:T(8,128)(2,1)} %param.13), channel_id=1, source_target_pairs={{0,64},{16,80},{32,96},{48,112},{64,128},{80,144},{96,160},{112,17... | collective-permute-start | bytes 294920 | tf_op jit(solution)/shard_map/ppermute | solution.py:12
  12.4 37.9 %collective-permute-start.2 = (bf16[48,8,128]{2,1,0:T(8,128)(2,1)}, bf16[48,8,128]{2,1,0:T(8,128)(2,1)S(1)}, u32[]{:S(2)}, u32[]{:S(2)}) collective-permute-start(bf16[48,8,128]{2,1,0:T(8,128)(2,1)} %param.13), channel_id=1, source_target_pairs={{0,48},{16,64},{32,80},{48,96},{64,112},{80,128},{96,144},{112,160... | collective-permute-start | bytes 294920 | tf_op jit(solution)/shard_map/ppermute | solution.py:12
  18.4 35.9 %collective-permute-start.3 = (bf16[48,8,128]{2,1,0:T(8,128)(2,1)}, bf16[48,8,128]{2,1,0:T(8,128)(2,1)S(1)}, u32[]{:S(2)}, u32[]{:S(2)}) collective-permute-start(bf16[48,8,128]{2,1,0:T(8,128)(2,1)} %param.13), channel_id=1, source_target_pairs={{0,32},{16,48},{32,64},{48,80},{64,96},{80,112},{96,128},{112,144}... | collective-permute-start | bytes 294920 | tf_op jit(solution)/shard_map/ppermute | solution.py:12
  24.2 15.3 %collective-permute-start = (bf16[48,4,128]{2,1,0:T(4,128)(2,1)S(1)}, bf16[48,4,128]{2,1,0:T(4,128)(2,1)S(1)}, u32[]{:S(2)}, u32[]{:S(2)}) collective-permute-start(bf16[48,4,128]{2,1,0:T(4,128)(2,1)S(1)} %get-tuple-element.19), channel_id=1, source_target_pairs={{0,80},{16,96},{32,112},{48,128},{64,144},{80,160},{96,176},{112,1... | collective-permute-start | bytes 147464 | tf_op jit(solution)/shard_map/ppermute | solution.py:12
  30.4 6.2 %copy-start.1 = (bf16[48,8,128]{2,1,0:T(8,128)(2,1)S(1)}, bf16[48,8,128]{2,1,0:T(8,128)(2,1)}, u32[]{:S(2)}) copy-start(bf16[48,8,128]{2,1,0:T(8,128)(2,1)} %param.13) | copy-start | bytes 294916
  30.4 11.6 %collective-permute-start.9 = (bf16[48,4,128]{2,1,0:T(4,128)(2,1)S(1)}, bf16[48,4,128]{2,1,0:T(4,128)(2,1)}, u32[]{:S(2)}, u32[]{:S(2)}) collective-permute-start(bf16[48,4,128]{2,1,0:T(4,128)(2,1)S(1)} %get-tuple-element.18), channel_id=1, source_target_pairs={{0,432},{16,448},{32,464},{48,480},{64,496},{80,0},{96,16},{112,32... | collective-permute-start | bytes 147464 | tf_op jit(solution)/shard_map/ppermute | solution.py:12
  39.5 20.2 %collective-permute-start.4 = (bf16[48,8,128]{2,1,0:T(8,128)(2,1)S(1)}, bf16[48,8,128]{2,1,0:T(8,128)(2,1)S(1)}, u32[]{:S(2)}, u32[]{:S(2)}) collective-permute-start(bf16[48,8,128]{2,1,0:T(8,128)(2,1)S(1)} %copy-done.1), channel_id=1, source_target_pairs={{0,16},{16,32},{32,48},{48,64},{64,80},{80,96},{96,112},{112,128},... | collective-permute-start | bytes 294920 | tf_op jit(solution)/shard_map/ppermute | solution.py:12
  42.1 17.7 %collective-permute-start.5 = (bf16[48,8,128]{2,1,0:T(8,128)(2,1)S(1)}, bf16[48,8,128]{2,1,0:T(8,128)(2,1)S(1)}, u32[]{:S(2)}, u32[]{:S(2)}) collective-permute-start(bf16[48,8,128]{2,1,0:T(8,128)(2,1)S(1)} %copy-done.1), channel_id=1, source_target_pairs={{0,496},{16,0},{32,16},{48,32},{64,48},{80,64},{96,80},{112,96},{1... | collective-permute-start | bytes 294920 | tf_op jit(solution)/shard_map/ppermute | solution.py:12
  48.4 11.4 %copy-start.9 = (bf16[48,8,128]{2,1,0:T(8,128)(2,1)}, bf16[48,8,128]{2,1,0:T(8,128)(2,1)S(1)}, u32[]{:S(2)}) copy-start(bf16[48,8,128]{2,1,0:T(8,128)(2,1)S(1)} %collective-permute-done.1) | copy-start | bytes 294916
  48.4 11.3 %collective-permute-start.6 = (bf16[48,8,128]{2,1,0:T(8,128)(2,1)S(1)}, bf16[48,8,128]{2,1,0:T(8,128)(2,1)S(1)}, u32[]{:S(2)}, u32[]{:S(2)}) collective-permute-start(bf16[48,8,128]{2,1,0:T(8,128)(2,1)S(1)} %copy-done.1), channel_id=1, source_target_pairs={{0,480},{16,496},{32,0},{48,16},{64,32},{80,48},{96,64},{112,80},{... | collective-permute-start | bytes 294920 | tf_op jit(solution)/shard_map/ppermute | solution.py:12
  50.3 9.4 %copy-start.15 = (bf16[48,8,128]{2,1,0:T(8,128)(2,1)}, bf16[48,8,128]{2,1,0:T(8,128)(2,1)S(1)}, u32[]{:S(2)}) copy-start(bf16[48,8,128]{2,1,0:T(8,128)(2,1)S(1)} %collective-permute-done.2) | copy-start | bytes 294916
  50.4 9.4 %collective-permute-start.7 = (bf16[48,8,128]{2,1,0:T(8,128)(2,1)S(1)}, bf16[48,8,128]{2,1,0:T(8,128)(2,1)S(1)}, u32[]{:S(2)}, u32[]{:S(2)}) collective-permute-start(bf16[48,8,128]{2,1,0:T(8,128)(2,1)S(1)} %copy-done.1), channel_id=1, source_target_pairs={{0,464},{16,480},{32,496},{48,0},{64,16},{80,32},{96,48},{112,64},... | collective-permute-start | bytes 294920 | tf_op jit(solution)/shard_map/ppermute | solution.py:12
  54.3 5.5 %copy-start.11 = (bf16[48,8,128]{2,1,0:T(8,128)(2,1)}, bf16[48,8,128]{2,1,0:T(8,128)(2,1)S(1)}, u32[]{:S(2)}) copy-start(bf16[48,8,128]{2,1,0:T(8,128)(2,1)S(1)} %collective-permute-done.3) | copy-start | bytes 294916
  54.3 10.5 %collective-permute-start.8 = (bf16[48,8,128]{2,1,0:T(8,128)(2,1)S(1)}, bf16[48,8,128]{2,1,0:T(8,128)(2,1)S(1)}, u32[]{:S(2)}, u32[]{:S(2)}) collective-permute-start(bf16[48,8,128]{2,1,0:T(8,128)(2,1)S(1)} %copy-done.1), channel_id=1, source_target_pairs={{0,448},{16,464},{32,480},{48,496},{64,0},{80,16},{96,32},{112,48}... | collective-permute-start | bytes 294920 | tf_op jit(solution)/shard_map/ppermute | solution.py:12
  59.7 0.6 copy-start.13
  59.7 0.7 copy-start.5
  60.4 0.6 copy-start.7
  80.7 0.9 copy-start.12
  80.7 0.9 copy-start.14
  80.7 1.1 copy-start.4
  81.6 0.9 copy-start.16
  81.8 1.0 copy-start.3
  82.5 0.9 copy-start.10
  82.8 1.0 copy-start.2
  83.5 0.9 copy-start.6
  84.4 0.9 copy-start.8
  86.5 1.3 copy-start.17
  86.5 1.5 copy-start.18
  87.8 135.9 %copy-start.20 = (bf16[5,256,16]{1,2,0:T(8,128)(2,1)S(1)}, bf16[5,256,16]{1,2,0:T(8,128)(2,1)}, u32[]{:S(2)}) copy-start(bf16[5,256,16]{1,2,0:T(8,128)(2,1)} %param.19) | copy-start | bytes 122884
  87.8 135.9 %copy-start.21 = (f32[5,256]{1,0:T(8,128)S(1)}, f32[5,256]{1,0:T(8,128)}, u32[]{:S(2)}) copy-start(f32[5,256]{1,0:T(8,128)} %param.18) | copy-start | bytes 15364
  87.8 135.9 %copy-start.22 = (f32[5,256]{1,0:T(8,128)S(1)}, f32[5,256]{1,0:T(8,128)}, u32[]{:S(2)}) copy-start(f32[5,256]{1,0:T(8,128)} %param.17) | copy-start | bytes 15364
  87.8 135.9 %copy-start.23 = (f32[16]{0:T(128)S(1)}, f32[16]{0:T(128)}, u32[]{:S(2)}) copy-start(f32[16]{0:T(128)} %param.21) | copy-start | bytes 196
  87.8 135.9 %copy-start.24 = (f32[16]{0:T(128)S(1)}, f32[16]{0:T(128)}, u32[]{:S(2)}) copy-start(f32[16]{0:T(128)} %param.20) | copy-start | bytes 196
  245.2 11.2 %collective-permute-start.10 = (bf16[48,1,304]{0,1,2:T(2,128)(2,1)S(1)}, bf16[48,1,304]{0,1,2:T(2,128)(2,1)S(1)}, u32[]{:S(2)}, u32[]{:S(2)}) collective-permute-start(bf16[48,1,304]{0,1,2:T(2,128)(2,1)S(1)} %get-tuple-element.8), channel_id=1, source_target_pairs={{0,16},{16,32},{32,48},{48,64},{64,80},{80,96},{96,112},{112,128},... | collective-permute-start | bytes 87560 | tf_op jit(solution)/shard_map/ppermute | solution.py:22
  248.9 11.3 %collective-permute-start.11 = (bf16[48,1,304]{0,1,2:T(2,128)(2,1)S(1)}, bf16[48,1,304]{0,1,2:T(2,128)(2,1)S(1)}, u32[]{:S(2)}, u32[]{:S(2)}) collective-permute-start(bf16[48,1,304]{0,1,2:T(2,128)(2,1)S(1)} %get-tuple-element.9), channel_id=1, source_target_pairs={{16,0},{32,16},{48,32},{64,48},{80,64},{96,80},{112,96},{128,112},... | collective-permute-start | bytes 87560 | tf_op jit(solution)/shard_map/ppermute | solution.py:23
  260.5 0.9 copy-start.19
  260.7 2.4 copy-start.25
  260.7 2.4 copy-start.26
Sparse Core Ops, SparseCore 0:
  88.0 135.6 all-reduce.3
where the time goes:
time: 273 us; the launch traced here: 271 us
  blocking collectives  123 us (45%)
  starting transfers between devices  56.4 us (21%)
  waiting for transfers between devices  40.2 us (15%)
  local copies, waits for them, and re-layouts  23.2 us (8%)
  between operations  14 us (5%)
  matrix products  12.4 us (5%)
    psum x1, blocking collectives, body(): image_total = lax.psum(image_part, ('lon', 'chan'))  104 us
    ppermute x10, starting transfers between devices, shifted(): return lax.ppermute(value, axis, pairs)  47.4 us
    psum x1, waiting for transfers between devices, body(): summed = lax.psum(partial_sums, 'chan')  31.6 us
    all_gather x1, blocking collectives, body(): pooled = lax.all_gather(pooled_own, 'chan', axis=2, tiled=True)  19 us
    concatenate x1, local copies, waits for them, and re-layouts, body(): wrapped = jnp.concatenate(west_parts + [features] + east_parts, axis=1)  13.3 us
    dot_general x36, matrix products, tap_sum(): jnp.dot(window.reshape(out_rows * out_cols, -1), weights[tap_row, tap_col...  10.3 us
  transfers between devices with their start and end apart: 13, of which 4 were waited for; matrix products, arithmetic and copies ran while one was open for 3% of the time, Pallas kernels for 0%

commit v1 on v0

v1 whole, which is shorter than its diff:
```python
import functools

import jax
import jax.numpy as jnp
from jax import lax
from jax.experimental import pallas as pl
from jax.experimental.pallas import tpu as pltpu
from jax.sharding import PartitionSpec as P

BF = jnp.bfloat16
F32 = jnp.float32
MESH = pl.DeviceIdType.MESH

ROWS, COLS, CH, BR, SK = 48, 8, 128, 256, 48
OWN = 3
RIM = 36
RATES = (2, 1, 0)
DIL = (12, 24, 36)
ORDERS = ((0, 2, 1), (2, 1, 0), (1, 0, 2))
LANES = ((0, 512), (512, 896), (896, 1280))
FAR = ((2, 1), (3, 3), (5, 4))
GRAY = ((0, 0), (0, 1), (1, 1), (1, 0))


def dot(a, b):
    return lax.dot_general(a, b, (((1,), (0,)), ((), ())), preferred_element_type=F32)


def dot_nt(a, b):
    return lax.dot_general(a, b, (((1,), (1,)), ((), ())), preferred_element_type=F32)


def to_tiles(v):
    n = v.shape[0] // 8
    lo = v[:, :128].reshape(n, 8, 128)
    hi = v[:, 128:].reshape(n, 8, 128)
    return jnp.concatenate([lo, hi], axis=1)


def from_tiles(t):
    n = t.shape[0]
    lo = t[:, :8].reshape(n * 8, 128)
    hi = t[:, 8:].reshape(n * 8, 128)
    return jnp.concatenate([lo, hi], axis=1)


class Several:
    def __init__(self):
        self.copies = []

    def wait(self):
        for cp in self.copies:
            cp.wait()


def kernel(
    n_lon,
    feat_h, wpt_h, wd_h, wpool_h, bns_h, bnt_h, pw_h, ps_h, pt_h, skip_h, mw_h, ms_h, mt_h,
    out_ref,
    feat, wpt, wd, wpool, bns, bnt, ps, pt, skip, ms, mt,
    xpad,
    acc0, sb0, r0, acc1, sb1, r1, acc2, sb2, r2, acc3, sb3, r3,
    pacc0, psb0, pr0, pacc1, psb1, pr1, pacc2, psb2, pr2, pacc3, psb3, pr3,
    fin, sh, rsh,
    wt0, wt1, wt2,
    ia, ib, ic, img,
    gat, wrow, wcat, vskip, proj, ev, rev,
    ld_sem, pw_sem, mw_sem,
    rs_s, rs_r, sh_s, sh_r, wt_s, wt_r, ia_s, ia_r, ib_s, ib_r, ic_s, ic_r, ga_s, ga_r, ev_s, ev_r,
):
    lon = lax.axis_index("lon")
    chan = lax.axis_index("chan")
    a = chan // 8
    y = (chan // 2) % 4
    c = chan % 2
    bit = (a, y // 2, (y % 2 + y // 2) % 2)
    beta = c * 8 + bit[0] * 4 + bit[1] * 2 + bit[2]

    loads = {}
    for i, (name, src, dst) in enumerate(
        [
            ("feat", feat_h, feat), ("wd2", wd_h.at[2], wd.at[2]), ("wd1", wd_h.at[1], wd.at[1]),
            ("wd0", wd_h.at[0], wd.at[0]), ("wpt", wpt_h, wpt), ("wpool", wpool_h, wpool),
            ("ps", ps_h, ps), ("pt", pt_h, pt), ("bns", bns_h, bns), ("bnt", bnt_h, bnt), ("skip", skip_h, skip),
            ("ms", ms_h, ms), ("mt", mt_h, mt),
        ]
    ):
        loads[name] = pltpu.make_async_copy(src, dst, ld_sem.at[i])
        loads[name].start()

    for p, ((s, e), ref) in enumerate(zip(LANES, (wt0, wt1, wt2))):
        loads[f"wt{p}"] = Several()
        for b in range(5):
            lo, hi = max(b * BR, s), min(b * BR + BR, e)
            if lo < hi:
                cp = pltpu.make_async_copy(
                    pw_h.at[b, :, lo - b * BR : hi - b * BR],
                    ref.at[bit[0], bit[1], bit[2], c, :, lo - s : hi - s],
                    pw_sem.at[p, b],
                )
                cp.start()
                loads[f"wt{p}"].copies.append(cp)
    loads["mw"] = Several()
    for t in range(3):
        for b in range(3):
            cp = pltpu.make_async_copy(mw_h.at[t, b], wrow.at[t, 16 * b : 16 * b + 16], mw_sem.at[t, b])
            cp.start()
            loads["mw"].copies.append(cp)

    def chan_peer(m):
        mc, mx, mh, ml = (m >> 3) & 1, (m >> 2) & 1, (m >> 1) & 1, m & 1
        pc = 1 - c if mc else c
        pa = 1 - a if mx else a
        flip = y + 1 - 2 * (y % 2)
        py = {(0, 0): y, (0, 1): flip, (1, 0): 3 - y, (1, 1): (y + 2) % 4}[(mh, ml)]
        return (lon, pa * 8 + py * 2 + pc)

    def beta_peer(m):
        bits = [c, *bit]
        masks = [(m >> 3) & 1, (m >> 2) & 1, (m >> 1) & 1, m & 1]
        f = [1 - b if k else b for b, k in zip(bits, masks)]
        return f[0] * 8 + f[1] * 4 + f[2] * 2 + f[3]

    sibling = chan_peer(8)
    step_peer = (chan_peer(4), chan_peer(2), chan_peer(1))

    def lon_peer(k):
        return ((lon + k + n_lon) % n_lon, chan)

    def lon_xor(m):
        out = lon
        for p in range(5):
            if (m >> p) & 1:
                b = (lon // (1 << p)) % 2
                out = out + (1 - 2 * b) * (1 << p)
        return (out, chan)

    near = list(range(1, 8))
    wide = [8 * m for m in range(1, n_lon // 8)]

    barrier = pltpu.get_barrier_semaphore()
    greeted = 0
    for dev in (
        [chan_peer(m) for m in range(1, 16)]
        + [lon_peer(k) for k in (1, 2, 3, 4, 5, -1, -2, -3, -4, -5)]
        + [lon_xor(m) for m in near + wide]
    ):
        pl.semaphore_signal(barrier, inc=1, device_id=dev, device_id_type=MESH)
        greeted += 1

    sends = []

    def send(src, dst, s, r, dev):
        cp = pltpu.make_async_remote_copy(
            src_ref=src, dst_ref=dst, send_sem=s, recv_sem=r, device_id=dev, device_id_type=MESH
        )
        cp.start()
        sends.append(cp)
        return cp

    A0, SB0, R0 = [acc0.at[0], acc0.at[1], acc0.at[2], pacc0], [sb0.at[0], sb0.at[1], sb0.at[2], psb0], [r0.at[0], r0.at[1], r0.at[2], pr0]
    ACC = [[acc1.at[k] for k in range(3)] + [pacc1], [acc2.at[k] for k in range(3)] + [pacc2], [acc3.at[k] for k in range(3)] + [pacc3]]
    SB = [[sb1.at[k] for k in range(3)] + [psb1], [sb2.at[k] for k in range(3)] + [psb2], [sb3.at[k] for k in range(3)] + [psb3]]
    RR = [[r1.at[k] for k in range(3)] + [pr1], [r2.at[k] for k in range(3)] + [pr2], [r3.at[k] for k in range(3)] + [pr3]]

    def put(k, p, tiles):
        t = tiles.reshape((2, 2, 2, 2) + tiles.shape[1:])
        A0[k][p] = t
        SB0[k][p] = t.astype(BF)

    def compute(k):
        if k < 3:
            rate = RATES[k]
            d = DIL[rate]
            loads[f"wd{rate}"].wait()
            lhs = jnp.concatenate(
                [xpad[(RIM + (t - 1) * d) * 8 : (RIM + (t - 1) * d + ROWS) * 8] for t in range(3)], axis=1
            )
            for tap in range(3):
                rhs = wd[rate, :, tap].reshape(3 * CH, BR)
                res = to_tiles(dot(lhs, rhs))
                put(k, tap, res.reshape(16, OWN, 16, 128))
        else:
            loads["wpt"].wait()
            res = to_tiles(dot(xpad[RIM * 8 : (RIM + ROWS) * 8], wpt[...])).reshape(16, OWN, 16, 128)
            for p in range(3):
                put(k, p, res[:, p : p + 1])

    pending = {}

    def core_send(k):
        pending[k, 0] = [
            send(SB0[k].at[p, 1 - c], R0[k].at[p], rs_s.at[k, 0, p], rs_r.at[k, 0, p], sibling) for p in range(3)
        ]

    def halve(k, step):
        sent = pending.pop((k, step))
        out = []
        for p in range(3):
            sent[p].wait_recv()
            left = [d for d in (0, 1, 2) if d not in ORDERS[p][:step]]
            mine = A0[k].at[p, c] if step == 0 else ACC[step - 1][k].at[p]
            got = R0[k].at[p] if step == 0 else RR[step - 1][k].at[p]
            d = ORDERS[p][step]

            def half(v):
                return tuple(v if q == d else slice(None) for q in left)

            there, here = half(1 - bit[d]), half(bit[d])
            shape = SB[step][k].shape[1:]
            SB[step][k][p] = (mine[there] + got[there].astype(F32)).astype(BF).reshape(shape)
            out.append(
                send(SB[step][k].at[p], RR[step][k].at[p], rs_s.at[k, step + 1, p], rs_r.at[k, step + 1, p], step_peer[d])
            )
            ACC[step][k][p] = (mine[here] + got[here].astype(F32)).reshape(shape)
        pending[k, step + 1] = out

    shifts = {}

    def finish(k):
        sent = pending.pop((k, 3))
        for p in (0, 2, 1):
            sent[p].wait_recv()
            v = ACC[2][k][p] + RR[2][k][p].astype(F32)
            if k == 3:
                fin[3, p : p + 1] = v
                continue
            if p == 1:
                fin[k] = v
                continue
            side, sign = (0, 1) if p == 0 else (1, -1)
            sh[k, side] = v.astype(BF)
            first, second = FAR[RATES[k]]
            if p == 2:
                first, second = second, first
            for j, dist in enumerate((first,) if first == second else (first, second)):
                shifts[k, side, j] = send(
                    sh.at[k, side], rsh.at[k, side, j], sh_s.at[k, side, j], sh_r.at[k, side, j], lon_peer(sign * dist)
                )

    def weights(l0, l1):
        parts = []
        for (s, e), ref in zip(LANES, (wt0, wt1, wt2)):
            lo, hi = max(l0, s), min(l1, e)
            if lo < hi:
                parts.append(
                    jnp.concatenate(
                        [ref[q, GRAY[v][0], GRAY[v][1], w, :, lo - s : hi - s] for q in (0, 1) for v in range(4) for w in (0, 1)],
                        axis=0,
                    )
                )
        return parts[0] if len(parts) == 1 else jnp.concatenate(parts, axis=1)

    def project(branch, value):
        act = jnp.maximum(value * bns[branch : branch + 1] + bnt[branch : branch + 1], 0.0)
        return dot_nt(act.astype(BF), weights(branch * BR, branch * BR + BR))

    def pad32(v):
        return jnp.concatenate([v, jnp.zeros((8, BR), F32)], axis=0)

    def branch_of(k):
        col = lax.broadcasted_iota(jnp.int32, (2 * OWN, 8, 128), 1)
        total = fin[k]
        for side in (0, 1):
            count = 1 if RATES[k] == 1 else 2
            tiles = []
            for j in range(count):
                shifts[k, side, j].wait_recv()
                tiles.append(rsh[k, side, j].astype(F32).reshape(2 * OWN, 8, 128))
            if count == 1:
                moved = tiles[0]
            else:
                moved = pltpu.roll(jnp.where(col >= 4, tiles[0], tiles[1]), 4, 1)
            total = total + moved.reshape(OWN, 16, 128)
        return project(1 + RATES[k], pad32(from_tiles(total)))

    WT = (wt0, wt1, wt2)
    wsent = {}

    def wt_step(step):
        for p in range(3):
            if step:
                wsent[step - 1, p].wait_recv()
            else:
                loads[f"wt{p}"].wait()
            done = ORDERS[p][:step]
            idx = tuple(slice(None) if d in done else bit[d] for d in range(3)) + (c,)
            ref = WT[p].at[idx]
            wsent[step, p] = send(ref, ref, wt_s.at[step, p], wt_r.at[step, p], step_peer[ORDERS[p][step]])

    def wt_core():
        for p in range(3):
            wsent[2, p].wait_recv()
            ref = WT[p].at[:, :, :, c]
            wsent[3, p] = send(ref, ref, wt_s.at[3, p], wt_r.at[3, p], sibling)

    isent = {}

    def image_start():
        loads["wpool"].wait()
        sums = jnp.sum(feat[...].astype(F32).reshape(ROWS * COLS, CH), axis=0, keepdims=True)
        hi = sums.astype(BF)
        rest = sums - hi.astype(F32)
        mid = rest.astype(BF)
        low = (rest - mid.astype(F32)).astype(BF)
        row = lax.broadcasted_iota(jnp.int32, (16, CH), 0)
        lhs = jnp.where(
            row == 0,
            hi.astype(F32),
            jnp.where(row == 1, mid.astype(F32), jnp.where(row == 2, low.astype(F32), 0.0)),
        ).astype(BF)
        ia[0] = jnp.sum(dot(lhs, wpool[...]), axis=0, keepdims=True)
        for m in near:
            isent[0, m] = send(ia.at[0], ia.at[m], ia_s.at[m], ia_r.at[m], lon_xor(m))

    def image_wide():
        for m in near:
            isent[0, m].wait_recv()
        total = ia[0]
        for m in near:
            total = total + ia[m]
        ib[0] = total
        for m in wide:
            isent[1, m] = send(ib.at[0], ib.at[m // 8], ib_s.at[m // 8], ib_r.at[m // 8], lon_xor(m))

    def image_chan():
        total = ib[0]
        for m in wide:
            isent[1, m].wait_recv()
            total = total + ib[m // 8]
        total = total / (ROWS * COLS * n_lon)
        loads["ps"].wait()
        loads["pt"].wait()
        lane = lax.broadcasted_iota(jnp.int32, (1, BR), 1) - chan * 16
        scale = jnp.zeros((1, BR), F32)
        shift = jnp.zeros((1, BR), F32)
        for i in range(16):
            scale = jnp.where(lane == i, ps[i], scale)
            shift = jnp.where(lane == i, pt[i], shift)
        ic[0, 0] = total
        ic[0, 1] = scale
        ic[0, 2] = shift
        for m in range(1, 16):
            isent[2, m] = send(ic.at[0], ic.at[m], ic_s.at[m], ic_r.at[m], chan_peer(m))

    def image_end():
        for m in range(1, 16):
            isent[2, m].wait_recv()
        total = ic[0]
        for m in range(1, 16):
            total = total + ic[m]
        img[...] = total

    def merge_prepare():
        loads["mw"].wait()
        loads["skip"].wait()
        wide_rows = (BR + SK, BR + SK)
        eye = (
            lax.broadcasted_iota(jnp.int32, wide_rows, 0) == lax.broadcasted_iota(jnp.int32, wide_rows, 1)
        ).astype(BF)
        for t in range(3):
            wrow[t, 48:] = jnp.zeros((80, BR + SK), BF)
            wcat[t] = dot_nt(eye, wrow[t]).astype(BF)
        s2 = skip[...].astype(F32).reshape(ROWS * COLS, SK).astype(BF)
        vskip[...] = rows_shifted([dot(s2, wcat[t, BR:]) for t in range(3)])

    def rows_shifted(parts):
        zero = jnp.zeros((8, 128), F32)
        n = ROWS * COLS
        up = jnp.concatenate([zero, parts[0][: n - 8]], axis=0)
        down = jnp.concatenate([parts[2][8:], zero], axis=0)
        return parts[1] + up + down

    loads["feat"].wait()
    x2 = feat[...].astype(F32).reshape(ROWS * COLS, CH).astype(BF)
    xpad[: RIM * 8] = jnp.zeros((RIM * 8, CH), BF)
    xpad[(RIM + ROWS) * 8 :] = jnp.zeros((RIM * 8, CH), BF)
    xpad[RIM * 8 : (RIM + ROWS) * 8] = x2
    compute(0)
    pl.semaphore_wait(barrier, greeted)
    core_send(0)
    compute(1)
    core_send(1)
    halve(0, 0)
    image_start()
    compute(2)
    core_send(2)
    halve(1, 0)
    wt_step(0)
    compute(3)
    core_send(3)
    halve(0, 1)
    halve(2, 0)
    image_wide()
    halve(1, 1)
    halve(3, 0)
    wt_step(1)
    halve(0, 2)
    image_chan()
    halve(2, 1)
    halve(3, 1)
    halve(1, 2)
    wt_step(2)
    merge_prepare()
    finish(0)
    halve(2, 2)
    halve(3, 2)
    finish(1)
    wt_core()
    finish(2)
    image_end()
    loads["bns"].wait()
    loads["bnt"].wait()
    for p in range(3):
        wsent[3, p].wait_recv()
    proj[...] = branch_of(0)
    proj[...] += project(4, jnp.broadcast_to(img[0], (32, BR)))
    proj[...] += branch_of(1)
    finish(3)
    proj[...] += project(0, pad32(from_tiles(fin[3])))
    pooled = proj[...] + branch_of(2)
    pooled = jnp.maximum(pooled * img[1] + img[2], 0.0)[: OWN * 8]
    gat[beta] = to_tiles(pooled).astype(BF)
    gsent = [send(gat.at[beta], gat.at[beta], ga_s.at[m], ga_r.at[m], chan_peer(m)) for m in range(1, 16)]
    for g in gsent:
        g.wait_recv()
    pf = from_tiles(gat[...].astype(F32).reshape(ROWS, 16, 128)).astype(BF)
    v = vskip[...] + rows_shifted([dot(pf, wcat[t, :BR]) for t in range(3)])
    vb = v.astype(BF)
    pick_r = lax.broadcasted_iota(jnp.int32, (ROWS, ROWS * COLS), 0)
    pick_c = lax.broadcasted_iota(jnp.int32, (ROWS, ROWS * COLS), 1)
    esent = []
    for i, (col, k) in enumerate(((7, 1), (0, -1))):
        ev[i] = dot((pick_c == pick_r * 8 + col).astype(BF), vb).astype(BF)
        esent.append(send(ev.at[i], rev.at[i], ev_s.at[i], ev_r.at[i], lon_peer(k)))
    v3 = v.reshape(ROWS, 8, 128)
    col = lax.broadcasted_iota(jnp.int32, (ROWS, 8, 128), 1)
    mid = pltpu.roll(v3, 112, 2)
    left = jnp.where(col == 0, 0.0, pltpu.roll(v3, 1, 1))
    right = jnp.where(col == 7, 0.0, pltpu.roll(pltpu.roll(v3, 96, 2), 7, 1))
    total = mid + left + right
    spread_r = lax.broadcasted_iota(jnp.int32, (ROWS * COLS, ROWS), 0)
    spread_c = lax.broadcasted_iota(jnp.int32, (ROWS * COLS, ROWS), 1)
    esent[0].wait_recv()
    esent[1].wait_recv()
    west = dot((spread_r == spread_c * 8).astype(BF), rev[0])
    east = dot((spread_r == spread_c * 8 + 7).astype(BF), rev[1])
    total = total + west.reshape(ROWS, 8, 128) + pltpu.roll(east.reshape(ROWS, 8, 128), 96, 2)
    loads["ms"].wait()
    loads["mt"].wait()
    lane = lax.broadcasted_iota(jnp.int32, (1, 1, 128), 2)
    scale = jnp.zeros((1, 1, 128), F32)
    shift = jnp.zeros((1, 1, 128), F32)
    for i in range(16):
        scale = jnp.where(lane == i, ms[i], scale)
        shift = jnp.where(lane == i, mt[i], shift)
    out_ref[...] = jnp.maximum(total * scale + shift, 0.0)[:, :, :16].astype(BF)
    for cp in sends:
        cp.wait_send()


def body(features, w_point, w_dilated, w_pool, bn_scale, bn_shift, proj_weight, proj_scale, proj_shift, skip, merge_weight, merge_scale, merge_shift):
    n_lon = lax.axis_size("lon")
    vm = pltpu.VMEM
    dma = pltpu.SemaphoreType.DMA
    t3, t1 = (OWN, 16, 128), (1, 16, 128)

    def steps(lead, t):
        shapes = [
            vm(lead + (3, 2, 2, 2, 2) + t, F32), vm(lead + (3, 2, 2, 2, 2) + t, BF), vm(lead + (3, 2, 2, 2) + t, BF),
        ]
        for rest in ((2, 2), (2,), ()):
            shapes += [vm(lead + (3,) + rest + t, F32), vm(lead + (3,) + rest + t, BF), vm(lead + (3,) + rest + t, BF)]
        return shapes

    scratch = (
        [
            vm((ROWS, COLS, CH), BF), vm((CH, BR), BF), vm((3, 3, 3, CH, BR), BF), vm((CH, BR), BF),
            vm((5, BR), F32), vm((5, BR), F32), pltpu.SMEM((16,), F32), pltpu.SMEM((16,), F32),
            vm((ROWS, COLS, SK), BF), pltpu.SMEM((16,), F32), pltpu.SMEM((16,), F32),
            vm(((ROWS + 2 * RIM) * 8, CH), BF),
        ]
        + steps((3,), t3)
        + steps((), t1)
        + [
            vm((4,) + t3, F32), vm((3, 2) + t3, BF), vm((3, 2, 2) + t3, BF),
            vm((2, 2, 2, 2, 16, 512), BF), vm((2, 2, 2, 2, 16, 384), BF), vm((2, 2, 2, 2, 16, 384), BF),
            vm((8, 1, BR), F32), vm((4, 1, BR), F32), vm((16, 3, 1, BR), F32), vm((3, 1, BR), F32),
            vm((16,) + t3, BF), vm((3, 128, BR + SK), BF), vm((3, BR + SK, 128), BF), vm((ROWS * COLS, 128), F32), vm((32, BR), F32),
            vm((2, ROWS, 128), BF), vm((2, ROWS, 128), BF),
            dma((13,)), dma((3, 5)), dma((3, 3)),
            dma((4, 4, 3)), dma((4, 4, 3)), dma((3, 2, 2)), dma((3, 2, 2)), dma((4, 3)), dma((4, 3)),
            dma((8,)), dma((8,)), dma((4,)), dma((4,)), dma((16,)), dma((16,)), dma((16,)), dma((16,)), dma((2,)), dma((2,)),
        ]
    )
    return pl.pallas_call(
        functools.partial(kernel, n_lon),
        out_shape=jax.ShapeDtypeStruct((ROWS, COLS, 16), BF),
        in_specs=[pl.BlockSpec(memory_space=pltpu.HBM)] * 13,
        out_specs=pl.BlockSpec(memory_space=pltpu.VMEM),
        scratch_shapes=scratch,
        compiler_params=pltpu.CompilerParams(
            collective_id=0, has_side_effects=True, vmem_limit_bytes=48 * 1024 * 1024
        ),
        name="aspp_head",
    )(features, w_point, w_dilated, w_pool, bn_scale, bn_shift, jnp.swapaxes(proj_weight, 1, 2), proj_scale, proj_shift, skip, jnp.swapaxes(merge_weight, 2, 3), merge_scale, merge_shift)


def solution(mesh):
    return jax.shard_map(
        body,
        mesh=mesh,
        in_specs=(
            P(None, "lon", "chan"),
            P("chan", None),
            P(None, None, None, "chan", None),
            P("chan", None),
            P(),
            P(),
            P(None, None, "chan"),
            P("chan"),
            P("chan"),
            P(None, "lon", None),
            P(None, None, None, "chan"),
            P("chan"),
            P("chan"),
        ),
        out_specs=P(None, "lon", "chan"),
        check_vma=False,
    )
```

time: 273 us -> 64.6 us (0.24)
  blocking collectives: 123 us -> 0 us
  starting transfers between devices: 56.4 us -> 0 us
  Pallas kernels: 0 us -> 52.7 us
  waiting for transfers between devices: 40.2 us -> 0 us
  between operations: 14 us -> 0.02 us
  matrix products: 12.4 us -> 0 us
  local copies, waits for them, and re-layouts: 23.2 us -> 11.4 us
    psum x1 -> x0, blocking collectives: 104 us -> none  [body(): image_total = lax.psum(image_part, ('lon', 'chan'))]
    ppermute x12 -> x0, starting transfers between devices: 56.4 us -> none  [the longest x10 47.4 us: shifted(): return lax.ppermute(value, axis, pairs)]
    pallas_call x0 -> x1, Pallas kernels: none -> 52.7 us  [body(): pl.pallas_call(functools.partial(kernel, n_lon), out_shape=jax.ShapeDtype...]
    psum x1 -> x0, waiting for transfers between devices: 31.6 us -> none  [body(): summed = lax.psum(partial_sums, 'chan')]
    all_gather x1 -> x0, blocking collectives: 19 us -> none  [body(): pooled = lax.all_gather(pooled_own, 'chan', axis=2, tiled=True)]
    concatenate x3 -> x0, local copies, waits for them, and re-layouts: 14.2 us -> none  [the longest x1 13.3 us: body(): wrapped = jnp.concatenate(west_parts + [features] + east_parts, axis=1)]
    dot_general x39 -> x0, matrix products: 12.4 us -> none  [the longest x36 10.3 us: tap_sum(): jnp.dot(window.reshape(out_rows * out_cols, -1), weights[tap_row, tap_col...]
    ppermute x12 -> x0, waiting for transfers between devices: 8.57 us -> none  [the longest x10 3.82 us: shifted(): return lax.ppermute(value, axis, pairs)]
  transfers between devices with their start and end apart: 13 -> 0, of which waited for: 4 -> 0; matrix products, arithmetic and copies ran while one was open for 3% -> 0% of each run, Pallas kernels for 0% -> 0%
where the time goes in v1:
time: 64.6 us; the launch traced here: 64.1 us
  Pallas kernels  52.7 us (82%)
  local copies, waits for them, and re-layouts  11.4 us (18%)
    pallas_call x1, Pallas kernels, body(): pl.pallas_call(functools.partial(kernel, n_lon), out_shape=jax.ShapeDtype...  52.7 us
    unnamed x26, local copies, waits for them, and re-layouts  10.6 us

profile of v1, /device:TPU:1, one launch (start us, length us, event | category | flops | bytes accessed | tf_op | source)
XLA Modules:
  0.0 64.1 jit_solution(3366899342019633805)
XLA Ops:
  0.0 0.0 copy-start
  0.0 1.5 %copy-done = bf16[3,3,3,128,256]{4,3,2,1,0:T(8,128)(2,1)S(1)} copy-done((bf16[3,3,3,128,256]{4,3,2,1,0:T(8,128)(2,1)S(1)}, bf16[3,3,3,128,256]{4,3,2,1,0:T(8,128)(2,1)}, u32[]{:S(2)}) %copy-start) | copy-done | bytes 1769496
  1.5 0.0 copy-start.1
  1.5 0.9 %copy-done.1 = bf16[3,3,304,16]{2,3,1,0:T(8,128)(2,1)S(1)} copy-done((bf16[3,3,304,16]{2,3,1,0:T(8,128)(2,1)S(1)}, bf16[3,3,304,16]{2,3,1,0:T(8,128)(2,1)}, u32[]{:S(2)}) %copy-start.1) | copy-done | bytes 87576
  2.4 0.0 copy-start.2
  2.4 0.9 %copy-done.2 = bf16[48,8,128]{2,1,0:T(8,128)(2,1)S(1)} copy-done((bf16[48,8,128]{2,1,0:T(8,128)(2,1)S(1)}, bf16[48,8,128]{2,1,0:T(8,128)(2,1)}, u32[]{:S(2)}) %copy-start.2) | copy-done | bytes 98328
  3.3 0.0 copy-start.3
  3.3 0.9 %copy-done.3 = bf16[48,8,48]{2,1,0:T(8,128)(2,1)S(1)} copy-done((bf16[48,8,48]{2,1,0:T(8,128)(2,1)S(1)}, bf16[48,8,48]{2,1,0:T(8,128)(2,1)}, u32[]{:S(2)}) %copy-start.3) | copy-done | bytes 36888
  4.2 0.0 copy-start.4
  4.2 0.8 %copy-done.4 = bf16[128,256]{1,0:T(8,128)(2,1)S(1)} copy-done((bf16[128,256]{1,0:T(8,128)(2,1)S(1)}, bf16[128,256]{1,0:T(8,128)(2,1)}, u32[]{:S(2)}) %copy-start.4) | copy-done | bytes 65560
  5.0 0.0 copy-start.5
  5.0 0.8 %copy-done.5 = bf16[128,256]{1,0:T(8,128)(2,1)S(1)} copy-done((bf16[128,256]{1,0:T(8,128)(2,1)S(1)}, bf16[128,256]{1,0:T(8,128)(2,1)}, u32[]{:S(2)}) %copy-start.5) | copy-done | bytes 65560
  5.8 0.0 copy-start.6
  5.8 0.8 %copy-done.6 = bf16[5,256,16]{1,2,0:T(8,128)(2,1)S(1)} copy-done((bf16[5,256,16]{1,2,0:T(8,128)(2,1)S(1)}, bf16[5,256,16]{1,2,0:T(8,128)(2,1)}, u32[]{:S(2)}) %copy-start.6) | copy-done | bytes 40984
  6.6 0.0 copy-start.7
  6.6 0.7 %copy-done.7 = f32[5,256]{1,0:T(8,128)S(1)} copy-done((f32[5,256]{1,0:T(8,128)S(1)}, f32[5,256]{1,0:T(8,128)}, u32[]{:S(2)}) %copy-start.7) | copy-done | bytes 5144
  7.3 0.0 copy-start.8
  7.3 0.7 %copy-done.8 = f32[5,256]{1,0:T(8,128)S(1)} copy-done((f32[5,256]{1,0:T(8,128)S(1)}, f32[5,256]{1,0:T(8,128)}, u32[]{:S(2)}) %copy-start.8) | copy-done | bytes 5144
  8.0 0.0 copy-start.9
  8.0 0.7 %copy-done.9 = f32[16]{0:T(128)S(1)} copy-done((f32[16]{0:T(128)S(1)}, f32[16]{0:T(128)}, u32[]{:S(2)}) %copy-start.9) | copy-done | bytes 88
  8.7 0.0 copy-start.10
  8.7 0.7 %copy-done.10 = f32[16]{0:T(128)S(1)} copy-done((f32[16]{0:T(128)S(1)}, f32[16]{0:T(128)}, u32[]{:S(2)}) %copy-start.10) | copy-done | bytes 88
  9.3 0.0 copy-start.11
  9.3 0.7 %copy-done.11 = f32[16]{0:T(128)S(1)} copy-done((f32[16]{0:T(128)S(1)}, f32[16]{0:T(128)}, u32[]{:S(2)}) %copy-start.11) | copy-done | bytes 88
  10.0 0.0 copy-start.12
  10.0 0.7 %copy-done.12 = f32[16]{0:T(128)S(1)} copy-done((f32[16]{0:T(128)S(1)}, f32[16]{0:T(128)}, u32[]{:S(2)}) %copy-start.12) | copy-done | bytes 88
  10.6 52.7 %aspp_head.1 = bf16[48,8,16]{2,1,0:T(8,128)(2,1)S(1)} custom-call(bf16[48,8,128]{2,1,0:T(8,128)(2,1)S(1)} %copy-done.2, bf16[128,256]{1,0:T(8,128)(2,1)S(1)} %copy-done.4, bf16[3,3,3,128,256]{4,3,2,1,0:T(8,128)(2,1)S(1)} %copy-done, bf16[128,256]{1,0:T(8,128)(2,1)S(1)} %copy-done.5, f32[5,256]{1,0:T(8,128)S(1)} %copy-done.7, f32[5,256]{1,0:T(8,128)S(1)} %copy-done.8, ...), custom_call_target="tpu_custom_call" | custom-call | tf_op jit(solution)/shard_map/aspp_head/pallas_call | solution.py:496
  63.4 0.7 %copy.14 = bf16[48,8,16]{0,2,1:T(8,128)(2,1)} copy(bf16[48,8,16]{2,1,0:T(8,128)(2,1)S(1)} %aspp_head.1) | data formatting | bytes 24576 | tf_op jit(solution)/shard_map/aspp_head/pallas_call | solution.py:496
Async XLA Ops:
  0.0 1.5 %copy-start = (bf16[3,3,3,128,256]{4,3,2,1,0:T(8,128)(2,1)S(1)}, bf16[3,3,3,128,256]{4,3,2,1,0:T(8,128)(2,1)}, u32[]{:S(2)}) copy-start(bf16[3,3,3,128,256]{4,3,2,1,0:T(8,128)(2,1)} %wd_h.1) | copy-start | bytes 5308420
  1.5 0.9 %copy-start.1 = (bf16[3,3,304,16]{2,3,1,0:T(8,128)(2,1)S(1)}, bf16[3,3,304,16]{2,3,1,0:T(8,128)(2,1)}, u32[]{:S(2)}) copy-start(bf16[3,3,304,16]{2,3,1,0:T(8,128)(2,1)} %param.23) | copy-start | bytes 262660
  2.4 0.9 %copy-start.2 = (bf16[48,8,128]{2,1,0:T(8,128)(2,1)S(1)}, bf16[48,8,128]{2,1,0:T(8,128)(2,1)}, u32[]{:S(2)}) copy-start(bf16[48,8,128]{2,1,0:T(8,128)(2,1)} %feat_h.1) | copy-start | bytes 294916
  3.3 0.9 %copy-start.3 = (bf16[48,8,48]{2,1,0:T(8,128)(2,1)S(1)}, bf16[48,8,48]{2,1,0:T(8,128)(2,1)}, u32[]{:S(2)}) copy-start(bf16[48,8,48]{2,1,0:T(8,128)(2,1)} %skip_h.1) | copy-start | bytes 110596
  4.2 0.8 %copy-start.4 = (bf16[128,256]{1,0:T(8,128)(2,1)S(1)}, bf16[128,256]{1,0:T(8,128)(2,1)}, u32[]{:S(2)}) copy-start(bf16[128,256]{1,0:T(8,128)(2,1)} %wpt_h.1) | copy-start | bytes 196612
  5.0 0.8 %copy-start.5 = (bf16[128,256]{1,0:T(8,128)(2,1)S(1)}, bf16[128,256]{1,0:T(8,128)(2,1)}, u32[]{:S(2)}) copy-start(bf16[128,256]{1,0:T(8,128)(2,1)} %wpool_h.1) | copy-start | bytes 196612
  5.8 0.8 %copy-start.6 = (bf16[5,256,16]{1,2,0:T(8,128)(2,1)S(1)}, bf16[5,256,16]{1,2,0:T(8,128)(2,1)}, u32[]{:S(2)}) copy-start(bf16[5,256,16]{1,2,0:T(8,128)(2,1)} %param.19) | copy-start | bytes 122884
  6.6 0.7 %copy-start.7 = (f32[5,256]{1,0:T(8,128)S(1)}, f32[5,256]{1,0:T(8,128)}, u32[]{:S(2)}) copy-start(f32[5,256]{1,0:T(8,128)} %bns_h.1) | copy-start | bytes 15364
  7.3 0.7 %copy-start.8 = (f32[5,256]{1,0:T(8,128)S(1)}, f32[5,256]{1,0:T(8,128)}, u32[]{:S(2)}) copy-start(f32[5,256]{1,0:T(8,128)} %bnt_h.1) | copy-start | bytes 15364
  8.0 0.7 %copy-start.9 = (f32[16]{0:T(128)S(1)}, f32[16]{0:T(128)}, u32[]{:S(2)}) copy-start(f32[16]{0:T(128)} %ps_h.1) | copy-start | bytes 196
  8.7 0.7 %copy-start.10 = (f32[16]{0:T(128)S(1)}, f32[16]{0:T(128)}, u32[]{:S(2)}) copy-start(f32[16]{0:T(128)} %pt_h.1) | copy-start | bytes 196
  9.3 0.7 %copy-start.11 = (f32[16]{0:T(128)S(1)}, f32[16]{0:T(128)}, u32[]{:S(2)}) copy-start(f32[16]{0:T(128)} %ms_h.1) | copy-start | bytes 196
  10.0 0.7 %copy-start.12 = (f32[16]{0:T(128)S(1)}, f32[16]{0:T(128)}, u32[]{:S(2)}) copy-start(f32[16]{0:T(128)} %mt_h.1) | copy-start | bytes 196

commit v2 on v1

v2 whole, which is shorter than its diff:
```python
import functools

import jax
import jax.numpy as jnp
from jax import lax
from jax.experimental import pallas as pl
from jax.experimental.pallas import tpu as pltpu
from jax.sharding import PartitionSpec as P

BF = jnp.bfloat16
F32 = jnp.float32
MESH = pl.DeviceIdType.MESH

ROWS, COLS, CH, BR, SK = 48, 8, 128, 256, 48
OWN = 3
RIM = 36
DIL = (12, 24, 36)
CHUNKS = (
    ((((2, 0), 0, 3),), (((2, 2), 0, 3),), (((1, 0), 0, 3),)),
    ((((1, 2), 0, 3),), (((0, 0), 0, 3),), (((0, 2), 0, 3),)),
    (
        (((2, 1), 0, 4), ("point", 0, 2)),
        (((1, 1), 0, 4), ("point", 2, 3)),
        (((0, 1), 0, 4), ("point", 3, 4)),
    ),
)
TILES = [[sum(hi - lo for _, lo, hi in part) for part in chunk] for chunk in CHUNKS]
ORDERS = ((0, 2, 1), (2, 1, 0), (1, 0, 2))
LANES = ((0, 512), (512, 896), (896, 1280))
FAR = {(0, 0): (2, 1), (0, 2): (1, 2), (1, 0): (3, 4, 2), (1, 2): (3, 2, 4), (2, 0): (5, 4), (2, 2): (4, 5)}
GRAY = ((0, 0), (0, 1), (1, 1), (1, 0))


def dot(a, b):
    return lax.dot_general(a, b, (((1,), (0,)), ((), ())), preferred_element_type=F32)


def dot_nt(a, b):
    return lax.dot_general(a, b, (((1,), (1,)), ((), ())), preferred_element_type=F32)


def to_tiles(v):
    n = v.shape[0] // 8
    lo = v[:, :128].reshape(n, 8, 128)
    hi = v[:, 128:].reshape(n, 8, 128)
    return jnp.concatenate([lo, hi], axis=1)


def from_tiles(t):
    n = t.shape[0]
    lo = t[:, :8].reshape(n * 8, 128)
    hi = t[:, 8:].reshape(n * 8, 128)
    return jnp.concatenate([lo, hi], axis=1)


class Several:
    def __init__(self):
        self.copies = []

    def wait(self):
        for cp in self.copies:
            cp.wait()


def kernel(
    n_lon,
    feat_h, wpt_h, wd_h, wpool_h, bns_h, bnt_h, pw_h, ps_h, pt_h, skip_h, mw_h, ms_h, mt_h,
    out_ref,
    *refs,
):
    (feat, wpt, wd, wpool, bns, bnt, ps, pt, skip, ms, mt, xs, xpad, hpad, edge, hedge), refs = refs[:16], refs[16:]
    steps, refs = refs[:108], refs[108:]
    (
        fin, sh, rsh, wt0, wt1, wt2, ia, ib, ic, img, gat, wrow, wcat, vskip, vskip_out, proj,
        ld_sem, pw_sem, mw_sem, known,
        rs_s, rs_r, sh_s, sh_r, wt_s, wt_r, ia_s, ia_r, ib_s, ib_r, ic_s, ic_r, ga_s, ga_r, ev_s, ev_r,
    ) = refs
    A0, SB0, R0 = ([[steps[(k * 3 + p) * 12 + i] for p in range(3)] for k in range(3)] for i in range(3))
    ACC, SB, RR = (
        [[[steps[(k * 3 + p) * 12 + 3 * (q + 1) + i] for p in range(3)] for k in range(3)] for q in range(3)] for i in range(3)
    )
    lon = lax.axis_index("lon")
    chan = lax.axis_index("chan")
    a = chan // 8
    y = (chan // 2) % 4
    c = chan % 2
    bit = (a, y // 2, (y % 2 + y // 2) % 2)
    beta = c * 8 + bit[0] * 4 + bit[1] * 2 + bit[2]

    loads = {}
    for i, (name, src, dst) in enumerate(
        [
            ("feat", feat_h, feat), ("wd2", wd_h.at[2], wd.at[2]), ("wd1", wd_h.at[1], wd.at[1]),
            ("wd0", wd_h.at[0], wd.at[0]), ("wpt", wpt_h, wpt), ("wpool", wpool_h, wpool),
            ("ps", ps_h, ps), ("pt", pt_h, pt), ("bns", bns_h, bns), ("bnt", bnt_h, bnt), ("skip", skip_h, skip),
            ("ms", ms_h, ms), ("mt", mt_h, mt),
        ]
    ):
        loads[name] = pltpu.make_async_copy(src, dst, ld_sem.at[i])
        loads[name].start()

    for p, ((s, e), ref) in enumerate(zip(LANES, (wt0, wt1, wt2))):
        loads[f"wt{p}"] = Several()
        for b in range(5):
            lo, hi = max(b * BR, s), min(b * BR + BR, e)
            if lo < hi:
                cp = pltpu.make_async_copy(
                    pw_h.at[b, :, lo - b * BR : hi - b * BR],
                    ref.at[bit[0], bit[1], bit[2], c, :, lo - s : hi - s],
                    pw_sem.at[p, b],
                )
                cp.start()
                loads[f"wt{p}"].copies.append(cp)
    loads["mw"] = Several()
    for t in range(3):
        for b in range(3):
            cp = pltpu.make_async_copy(mw_h.at[t, b], wrow.at[t, 16 * b : 16 * b + 16], mw_sem.at[t, b])
            cp.start()
            loads["mw"].copies.append(cp)

    def chan_peer(m):
        mc, mx, mh, ml = (m >> 3) & 1, (m >> 2) & 1, (m >> 1) & 1, m & 1
        pc = 1 - c if mc else c
        pa = 1 - a if mx else a
        flip = y + 1 - 2 * (y % 2)
        py = {(0, 0): y, (0, 1): flip, (1, 0): 3 - y, (1, 1): (y + 2) % 4}[(mh, ml)]
        return (lon, pa * 8 + py * 2 + pc)

    def beta_peer(m):
        bits = [c, *bit]
        masks = [(m >> 3) & 1, (m >> 2) & 1, (m >> 1) & 1, m & 1]
        f = [1 - b if k else b for b, k in zip(bits, masks)]
        return f[0] * 8 + f[1] * 4 + f[2] * 2 + f[3]

    sibling = chan_peer(8)
    step_peer = (chan_peer(4), chan_peer(2), chan_peer(1))

    def lon_peer(k):
        return ((lon + k + n_lon) % n_lon, chan)

    def lon_xor(m):
        out = lon
        for p in range(5):
            if (m >> p) & 1:
                b = (lon // (1 << p)) % 2
                out = out + (1 - 2 * b) * (1 << p)
        return (out, chan)

    near = list(range(1, 8))
    blocks = n_lon // 8

    barrier = pltpu.get_barrier_semaphore()
    greeted = 0
    for dev in (
        [chan_peer(m) for m in range(1, 16)]
        + [lon_peer(k) for k in (1, 2, 3, 4, 5, -1, -2, -3, -4, -5)]
        + [lon_xor(m) for m in near]
        + ([lon_peer(8), lon_peer(-8)] if blocks > 1 else [])
    ):
        pl.semaphore_signal(barrier, inc=1, device_id=dev, device_id_type=MESH)
        greeted += 1

    sends = []

    def send(src, dst, s, r, dev):
        cp = pltpu.make_async_remote_copy(
            src_ref=src, dst_ref=dst, send_sem=s, recv_sem=r, device_id=dev, device_id_type=MESH
        )
        cp.start()
        sends.append(cp)
        return cp

    def taps(ref, d):
        return jnp.concatenate([ref[(RIM + (t - 1) * d) * 8 : (RIM + (t - 1) * d + ROWS) * 8] for t in range(3)], axis=1)

    def field(which, ref):
        if which == "point":
            return to_tiles(dot(ref[RIM * 8 : (RIM + ROWS) * 8], wpt[...])).reshape(16, OWN, 16, 128)
        rate, tap = which
        res = dot(taps(ref, DIL[rate]), wd[rate, :, tap].reshape(3 * CH, BR))
        return to_tiles(res).reshape(16, OWN, 16, 128)

    def whole(which, outer):
        main = field(which, xpad)
        if not outer:
            return main
        rim = field(which, hpad).reshape(16, OWN, 2, 8, 128)
        last = rim[:, 0] + sum(
            pltpu.roll(rim[:, j].reshape(32, 8, 128), 2 * j, 1).reshape(16, 2, 8, 128) for j in range(1, OWN)
        )
        return jnp.concatenate([main, last.reshape(16, 1, 16, 128)], axis=1)

    def compute(k):
        made = {}
        for p in range(3):
            at = 0
            for which, lo, hi in CHUNKS[k][p]:
                if which not in made:
                    made[which] = whole(which, k == 2)
                t = made[which][:, lo:hi].reshape(2, 2, 2, 2, hi - lo, 16, 128)
                A0[k][p][:, :, :, :, at : at + hi - lo] = t
                SB0[k][p][:, :, :, :, at : at + hi - lo] = t.astype(BF)
                at += hi - lo

    pending = {}

    def core_send(k):
        pending[k, 0] = [
            send(SB0[k][p].at[1 - c], R0[k][p], rs_s.at[k, 0, p], rs_r.at[k, 0, p], sibling) for p in range(3)
        ]

    def halve(k, step):
        sent = pending.pop((k, step))
        out = []
        for p in range(3):
            sent[p].wait_recv()
            left = [d for d in (0, 1, 2) if d not in ORDERS[p][:step]]
            mine = A0[k][p].at[c] if step == 0 else ACC[step - 1][k][p]
            got = R0[k][p] if step == 0 else RR[step - 1][k][p]
            d = ORDERS[p][step]

            def half(v):
                return tuple(v if q == d else slice(None) for q in left)

            there, here = half(1 - bit[d]), half(bit[d])
            SB[step][k][p][...] = (mine[there] + got[there].astype(F32)).astype(BF)
            out.append(
                send(SB[step][k][p], RR[step][k][p], rs_s.at[k, step + 1, p], rs_r.at[k, step + 1, p], step_peer[d])
            )
            ACC[step][k][p][...] = mine[here] + got[here].astype(F32)
        pending[k, step + 1] = out

    shifts = {}

    def finish(k):
        sent = pending.pop((k, 3))
        for p in range(3):
            sent[p].wait_recv()
            v = ACC[2][k][p][...] + RR[2][k][p][...].astype(F32)
            at = 0
            for which, lo, hi in CHUNKS[k][p]:
                part = v[at : at + hi - lo]
                at += hi - lo
                if which == "point":
                    fin[3, lo:hi] = part
                elif which[1] == 1:
                    fin[which[0]] = part
                else:
                    rate, tap = which
                    side, sign = (0, 1) if tap == 0 else (1, -1)
                    sh[rate, side] = part.astype(BF)
                    for j, dist in enumerate(FAR[which]):
                        shifts[rate, side, j] = send(
                            sh.at[rate, side], rsh.at[rate, side, j], sh_s.at[rate, side, j], sh_r.at[rate, side, j],
                            lon_peer(sign * dist),
                        )

    def weights(l0, l1):
        parts = []
        for (s, e), ref in zip(LANES, (wt0, wt1, wt2)):
            lo, hi = max(l0, s), min(l1, e)
            if lo < hi:
                parts.append(
                    jnp.concatenate(
                        [ref[q, GRAY[v][0], GRAY[v][1], w, :, lo - s : hi - s] for q in (0, 1) for v in range(4) for w in (0, 1)],
                        axis=0,
                    )
                )
        return parts[0] if len(parts) == 1 else jnp.concatenate(parts, axis=1)

    def project(branch, value):
        act = jnp.maximum(value * bns[branch : branch + 1] + bnt[branch : branch + 1], 0.0)
        return dot_nt(act.astype(BF), weights(branch * BR, branch * BR + BR))

    def branch_of(rate):
        sub = lax.broadcasted_iota(jnp.int32, (2, 8, 128), 1)
        col = lax.broadcasted_iota(jnp.int32, (2 * OWN, 8, 128), 1)
        total = fin[rate]
        for side, tap in ((0, 0), (1, 2)):
            tiles = []
            for j in range(len(FAR[rate, tap])):
                shifts[rate, side, j].wait_recv()
                tiles.append(rsh[rate, side, j].astype(F32).reshape(OWN, 2, 8, 128))
            if rate == 1:
                moved = tiles[0].reshape(OWN, 16, 128)
                west, east, w_col, e_col = tiles[1], tiles[2], 7, 0
            else:
                flat = [t.reshape(2 * OWN, 8, 128) for t in tiles]
                moved = pltpu.roll(jnp.where(col >= 4, flat[0], flat[1]), 4, 1).reshape(OWN, 16, 128)
                west, east, w_col, e_col = tiles[0], tiles[1], 3, 4
            rim = jnp.zeros((2, 8, 128), F32)
            for j in range(OWN):
                rim = jnp.where(sub == 2 * j, pltpu.roll(west[j], (2 * j - w_col) % 8, 1), rim)
                rim = jnp.where(sub == 2 * j + 1, pltpu.roll(east[j], (2 * j + 1 - e_col) % 8, 1), rim)
            total = total + jnp.concatenate([moved, rim.reshape(1, 16, 128)], axis=0)
        return project(1 + rate, from_tiles(total))

    WT = (wt0, wt1, wt2)
    wsent = {}

    def wt_step(step):
        for p in range(3):
            if step:
                wsent[step - 1, p].wait_recv()
            else:
                loads[f"wt{p}"].wait()
            done = ORDERS[p][:step]
            idx = tuple(slice(None) if d in done else bit[d] for d in range(3)) + (c,)
            ref = WT[p].at[idx]
            wsent[step, p] = send(ref, ref, wt_s.at[step, p], wt_r.at[step, p], step_peer[ORDERS[p][step]])

    def wt_core():
        for p in range(3):
            wsent[2, p].wait_recv()
            ref = WT[p].at[:, :, :, c]
            wsent[3, p] = send(ref, ref, wt_s.at[3, p], wt_r.at[3, p], sibling)

    isent = {}

    def image_start():
        loads["wpool"].wait()
        sums = jnp.sum(feat[...].astype(F32).reshape(ROWS * COLS, CH), axis=0, keepdims=True)
        hi = sums.astype(BF)
        rest = sums - hi.astype(F32)
        mid = rest.astype(BF)
        low = (rest - mid.astype(F32)).astype(BF)
        row = lax.broadcasted_iota(jnp.int32, (16, CH), 0)
        lhs = jnp.where(
            row == 0,
            hi.astype(F32),
            jnp.where(row == 1, mid.astype(F32), jnp.where(row == 2, low.astype(F32), 0.0)),
        ).astype(BF)
        loads["ps"].wait()
        loads["pt"].wait()
        lane = lax.broadcasted_iota(jnp.int32, (1, BR), 1) - chan * 16
        scale = jnp.zeros((1, BR), F32)
        shift = jnp.zeros((1, BR), F32)
        for i in range(16):
            scale = jnp.where(lane == i, ps[i], scale)
            shift = jnp.where(lane == i, pt[i], shift)
        ic[0, 0] = jnp.sum(dot(lhs, wpool[...]), axis=0, keepdims=True)
        ic[0, 1] = scale
        ic[0, 2] = shift

    def image_send():
        for m in range(1, 16):
            isent[2, m] = send(ic.at[0], ic.at[m], ic_s.at[m], ic_r.at[m], chan_peer(m))

    def image_near():
        for m in range(1, 16):
            isent[2, m].wait_recv()
        total = ic[0]
        for m in range(1, 16):
            total = total + ic[m]
        img[...] = total
        ia[0] = total[0]
        for m in near:
            isent[0, m] = send(ia.at[0], ia.at[m], ia_s.at[m], ia_r.at[m], lon_xor(m))

    def image_wide():
        for m in near:
            isent[0, m].wait_recv()
        total = ia[0]
        for m in near:
            total = total + ia[m]
        ib[0] = total
        if blocks > 1:
            pl.semaphore_wait(known, 1)
            for m in range(1, blocks):
                isent[1, m] = send(ib.at[0], ib.at[m], ib_s.at[m], ib_r.at[m], lon_peer(8 * m))

    def image_end():
        total = ib[0]
        for m in range(1, blocks):
            isent[1, m].wait_recv()
            total = total + ib[m]
        return total / (ROWS * COLS * n_lon)

    def tell_known():
        if blocks > 1:
            pl.semaphore_signal(known, inc=1, device_id=lon_peer(-8), device_id_type=MESH)

    esent = []

    def edge_send():
        loads["skip"].wait()
        xs[...] = jnp.zeros((ROWS * COLS, 2 * CH), BF)
        xs[:, :CH] = x2
        xs[:, CH : CH + SK] = skip[...].astype(F32).reshape(ROWS * COLS, SK).astype(BF)
        pick_r = lax.broadcasted_iota(jnp.int32, (ROWS, ROWS * COLS), 0)
        pick_c = lax.broadcasted_iota(jnp.int32, (ROWS, ROWS * COLS), 1)
        for i, col in enumerate((7, 0)):
            edge[i] = dot((pick_c == pick_r * 8 + col).astype(BF), xs[...]).astype(BF)

    def edge_start():
        for i, k in enumerate((1, -1)):
            esent.append(send(edge.at[i], hedge.at[i], ev_s.at[i], ev_r.at[i], lon_peer(k)))

    def edge_place():
        for e in esent:
            e.wait_recv()
        spread_r = lax.broadcasted_iota(jnp.int32, (ROWS * COLS, ROWS), 0)
        spread_c = lax.broadcasted_iota(jnp.int32, (ROWS * COLS, ROWS), 1)
        placed = sum(dot((spread_r == spread_c * 8 + i).astype(BF), hedge[i, :, :CH]) for i in range(2))
        hpad[RIM * 8 : (RIM + ROWS) * 8] = placed.astype(BF)

    def merge_prepare():
        loads["mw"].wait()
        wide_rows = (BR + SK, BR + SK)
        eye = (
            lax.broadcasted_iota(jnp.int32, wide_rows, 0) == lax.broadcasted_iota(jnp.int32, wide_rows, 1)
        ).astype(BF)
        for t in range(3):
            wrow[t, 48:] = jnp.zeros((80, BR + SK), BF)
            wcat[t] = dot_nt(eye, wrow[t]).astype(BF)
        vskip[...] = rows_shifted([dot(xs[:, CH : CH + SK], wcat[t, BR:]) for t in range(3)])
        spread_r = lax.broadcasted_iota(jnp.int32, (ROWS * COLS, ROWS), 0)
        spread_c = lax.broadcasted_iota(jnp.int32, (ROWS * COLS, ROWS), 1)
        outer = dot((spread_r == spread_c * 8 + 7).astype(BF), hedge[0, :, CH:]) + dot(
            (spread_r == spread_c * 8).astype(BF), hedge[1, :, CH:]
        )
        outer = outer[:, :SK].astype(BF)
        vskip_out[...] = rows_shifted([dot(outer, wcat[t, BR:]) for t in range(3)])

    def rows_shifted(parts):
        zero = jnp.zeros((8, 128), F32)
        n = ROWS * COLS
        up = jnp.concatenate([zero, parts[0][: n - 8]], axis=0)
        down = jnp.concatenate([parts[2][8:], zero], axis=0)
        return parts[1] + up + down

    loads["feat"].wait()
    x2 = feat[...].astype(F32).reshape(ROWS * COLS, CH).astype(BF)
    xpad[: RIM * 8] = jnp.zeros((RIM * 8, CH), BF)
    xpad[(RIM + ROWS) * 8 :] = jnp.zeros((RIM * 8, CH), BF)
    hpad[: RIM * 8] = jnp.zeros((RIM * 8, CH), BF)
    hpad[(RIM + ROWS) * 8 :] = jnp.zeros((RIM * 8, CH), BF)
    xpad[RIM * 8 : (RIM + ROWS) * 8] = x2
    image_start()
    edge_send()
    loads["wd2"].wait()
    loads["wd1"].wait()
    compute(0)
    pl.semaphore_wait(barrier, greeted)
    core_send(0)
    edge_start()
    image_send()
    tell_known()
    loads["wd0"].wait()
    compute(1)
    core_send(1)
    halve(0, 0)
    wt_step(0)
    halve(1, 0)
    loads["wpt"].wait()
    halve(0, 1)
    halve(1, 1)
    edge_place()
    compute(2)
    core_send(2)
    image_near()
    halve(0, 2)
    halve(2, 0)
    halve(1, 2)
    wt_step(1)
    finish(0)
    finish(1)
    halve(2, 1)
    image_wide()
    wt_step(2)
    merge_prepare()
    halve(2, 2)
    wt_core()
    loads["bns"].wait()
    loads["bnt"].wait()
    loads["ms"].wait()
    loads["mt"].wait()
    finish(2)
    for p in range(3):
        wsent[3, p].wait_recv()
    proj[...] = project(0, from_tiles(fin[3]))
    proj[...] += branch_of(2)
    proj[...] += branch_of(1)
    proj[...] += branch_of(0)
    gat[beta] = to_tiles(proj[...]).astype(BF)
    gsent = [send(gat.at[beta], gat.at[beta], ga_s.at[m], ga_r.at[m], chan_peer(m)) for m in range(1, 16)]
    offset = project(4, jnp.broadcast_to(image_end(), (32, BR)))[:8]
    for g in gsent:
        g.wait_recv()

    def on_tiles(v):
        return to_tiles(jnp.broadcast_to(v, (8, BR)))[None]

    pooled = jnp.maximum((gat[...].astype(F32) + on_tiles(offset)) * on_tiles(img[1]) + on_tiles(img[2]), 0.0)
    pf = from_tiles(pooled[:, :OWN].reshape(ROWS, 16, 128)).astype(BF)
    rim = from_tiles(pooled[:, OWN]).astype(BF)
    v = vskip[...] + rows_shifted([dot(pf, wcat[t, :BR]) for t in range(3)])
    cell = lax.broadcasted_iota(jnp.int32, (ROWS * COLS, 128), 0)
    held = lax.broadcasted_iota(jnp.int32, (ROWS * COLS, 128), 1)
    row = cell // 8
    west_at = (row // OWN) * 8 + 2 * (row % OWN)
    take = ((cell % 8 == 7) & (held == west_at)) | ((cell % 8 == 0) & (held == west_at + 1))
    outer = dot(take.astype(BF), rim).astype(BF)
    vo = vskip_out[...] + rows_shifted([dot(outer, wcat[t, :BR]) for t in range(3)])
    v3 = v.reshape(ROWS, 8, 128)
    vo3 = vo.reshape(ROWS, 8, 128)
    col = lax.broadcasted_iota(jnp.int32, (ROWS, 8, 128), 1)
    mid = pltpu.roll(v3, 112, 2)
    left = pltpu.roll(jnp.where(col == 7, vo3, v3), 1, 1)
    right = pltpu.roll(pltpu.roll(jnp.where(col == 0, vo3, v3), 96, 2), 7, 1)
    total = mid + left + right
    lane = lax.broadcasted_iota(jnp.int32, (1, 1, 128), 2)
    scale = jnp.zeros((1, 1, 128), F32)
    shift = jnp.zeros((1, 1, 128), F32)
    for i in range(16):
        scale = jnp.where(lane == i, ms[i], scale)
        shift = jnp.where(lane == i, mt[i], shift)
    out_ref[...] = jnp.maximum(total * scale + shift, 0.0)[:, :, :16].astype(BF)
    for cp in sends:
        cp.wait_send()


def body(features, w_point, w_dilated, w_pool, bn_scale, bn_shift, proj_weight, proj_scale, proj_shift, skip, merge_weight, merge_scale, merge_shift):
    n_lon = lax.axis_size("lon")
    vm = pltpu.VMEM
    dma = pltpu.SemaphoreType.DMA
    t3, t4 = (OWN, 16, 128), (OWN + 1, 16, 128)
    steps = []
    for chunk in TILES:
        for n in chunk:
            for i, rest in enumerate(((2, 2, 2), (2, 2), (2,), ())):
                own = ((2,) + rest if i == 0 else rest) + (n, 16, 128)
                steps += [vm(own, F32), vm(own, BF), vm(rest + (n, 16, 128), BF)]
    scratch = (
        [
            vm((ROWS, COLS, CH), BF), vm((CH, BR), BF), vm((3, 3, 3, CH, BR), BF), vm((CH, BR), BF),
            vm((5, BR), F32), vm((5, BR), F32), pltpu.SMEM((16,), F32), pltpu.SMEM((16,), F32),
            vm((ROWS, COLS, SK), BF), pltpu.SMEM((16,), F32), pltpu.SMEM((16,), F32),
            vm((ROWS * COLS, 2 * CH), BF), vm(((ROWS + 2 * RIM) * 8, CH), BF), vm(((ROWS + 2 * RIM) * 8, CH), BF),
            vm((2, ROWS, 2 * CH), BF), vm((2, ROWS, 2 * CH), BF),
        ]
        + steps
        + [
            vm((4,) + t4, F32), vm((3, 2) + t3, BF), vm((3, 2, 3) + t3, BF),
            vm((2, 2, 2, 2, 16, 512), BF), vm((2, 2, 2, 2, 16, 384), BF), vm((2, 2, 2, 2, 16, 384), BF),
            vm((8, 1, BR), F32), vm((4, 1, BR), F32), vm((16, 3, 1, BR), F32), vm((3, 1, BR), F32),
            vm((16,) + t4, BF), vm((3, 128, BR + SK), BF), vm((3, BR + SK, 128), BF),
            vm((ROWS * COLS, 128), F32), vm((ROWS * COLS, 128), F32), vm((32, BR), F32),
            dma((13,)), dma((3, 5)), dma((3, 3)), pltpu.SemaphoreType.REGULAR,
            dma((3, 4, 3)), dma((3, 4, 3)), dma((3, 2, 3)), dma((3, 2, 3)), dma((4, 3)), dma((4, 3)),
            dma((8,)), dma((8,)), dma((4,)), dma((4,)), dma((16,)), dma((16,)), dma((16,)), dma((16,)), dma((2,)), dma((2,)),
        ]
    )
    return pl.pallas_call(
        functools.partial(kernel, n_lon),
        out_shape=jax.ShapeDtypeStruct((ROWS, COLS, 16), BF),
        in_specs=[pl.BlockSpec(memory_space=pltpu.HBM)] * 13,
        out_specs=pl.BlockSpec(memory_space=pltpu.VMEM),
        scratch_shapes=scratch,
        compiler_params=pltpu.CompilerParams(
            collective_id=0, has_side_effects=True, vmem_limit_bytes=63 * 1024 * 1024
        ),
        name="aspp_head",
    )(features, w_point, w_dilated, w_pool, bn_scale, bn_shift, jnp.swapaxes(proj_weight, 1, 2), proj_scale, proj_shift, skip, jnp.swapaxes(merge_weight, 2, 3), merge_scale, merge_shift)


def solution(mesh):
    return jax.shard_map(
        body,
        mesh=mesh,
        in_specs=(
            P(None, "lon", "chan"),
            P("chan", None),
            P(None, None, None, "chan", None),
            P("chan", None),
            P(),
            P(),
            P(None, None, "chan"),
            P("chan"),
            P("chan"),
            P(None, "lon", None),
            P(None, None, None, "chan"),
            P("chan"),
            P("chan"),
        ),
        out_specs=P(None, "lon", "chan"),
        check_vma=False,
    )
```

time: 64.6 us -> 47.8 us (0.74)
  local copies, waits for them, and re-layouts: 11.4 us -> 1.61 us
  Pallas kernels: 52.7 us -> 46 us
    unnamed x26 -> x0, local copies, waits for them, and re-layouts: 10.6 us -> none
    pallas_call x1, Pallas kernels: 52.7 us -> 46 us  [body(): pl.pallas_call(functools.partial(kernel, n_lon), out_shape=jax.ShapeDtype...]
    pallas_call x1, local copies, waits for them, and re-layouts: 0.73 us -> 1.61 us  [body(): pl.pallas_call(functools.partial(kernel, n_lon), out_shape=jax.ShapeDtype...]
where the time goes in v2:
time: 47.8 us; the launch traced here: 47.6 us
  Pallas kernels  46 us (96%)
  local copies, waits for them, and re-layouts  1.61 us (3%)
    pallas_call x1, Pallas kernels, body(): pl.pallas_call(functools.partial(kernel, n_lon), out_shape=jax.ShapeDtype...  46 us
    pallas_call x1, local copies, waits for them, and re-layouts, body(): pl.pallas_call(functools.partial(kernel, n_lon), out_shape=jax.ShapeDtype...  1.61 us

profile of v2, /device:TPU:1, one launch (start us, length us, event | category | flops | bytes accessed | tf_op | source)
XLA Modules:
  0.0 47.6 jit_solution(10465630802469479458)
XLA Ops:
  0.0 46.0 %aspp_head.1 = bf16[48,8,16]{2,1,0:T(8,128)(2,1)} custom-call(bf16[48,8,128]{2,1,0:T(8,128)(2,1)} %feat_h.1, bf16[128,256]{1,0:T(8,128)(2,1)} %wpt_h.1, bf16[3,3,3,128,256]{4,3,2,1,0:T(8,128)(2,1)} %wd_h.1, bf16[128,256]{1,0:T(8,128)(2,1)} %wpool_h.1, f32[5,256]{1,0:T(8,128)} %bns_h.1, f32[5,256]{1,0:T(8,128)} %bnt_h.1, bf16[5,16,256]{2,1,0:T(8,128)(2,1)} %bitcast.3, ...), custom_call_target="tpu_custom_call" | custom-call | tf_op jit(solution)/shard_map/aspp_head/pallas_call | solution.py:554
  46.0 1.6 %copy.14 = bf16[48,8,16]{0,2,1:T(8,128)(2,1)} copy(bf16[48,8,16]{2,1,0:T(8,128)(2,1)} %aspp_head.1) | data formatting | bytes 24576 | tf_op jit(solution)/shard_map/aspp_head/pallas_call | solution.py:554

commit v3 on v2

--- a/solution.py
+++ b/solution.py
@@ -19,9 +19,9 @@
     ((((2, 0), 0, 3),), (((2, 2), 0, 3),), (((1, 0), 0, 3),)),
     ((((1, 2), 0, 3),), (((0, 0), 0, 3),), (((0, 2), 0, 3),)),
     (
-        (((2, 1), 0, 4), ("point", 0, 2)),
-        (((1, 1), 0, 4), ("point", 2, 3)),
-        (((0, 1), 0, 4), ("point", 3, 4)),
+        (((2, 1), 0, 3), ("point", 0, 1)),
+        (((1, 1), 0, 3), ("point", 1, 2)),
+        (((0, 1), 0, 3), ("point", 2, 3)),
     ),
 )
 TILES = [[sum(hi - lo for _, lo, hi in part) for part in chunk] for chunk in CHUNKS]
@@ -73,7 +73,7 @@
     (
         fin, sh, rsh, wt0, wt1, wt2, ia, ib, ic, img, gat, wrow, wcat, vskip, vskip_out, proj,
         ld_sem, pw_sem, mw_sem, known,
-        rs_s, rs_r, sh_s, sh_r, wt_s, wt_r, ia_s, ia_r, ib_s, ib_r, ic_s, ic_r, ga_s, ga_r, ev_s, ev_r,
+        rs_s, rs_r, sh_s, sh_r, wt_s, wt_r, ia_s, ia_r, ib_s, ib_r, ic_s, ic_r, ga_s, ga_r, ev_s, ev_r, hb, hbs, hr, hr_s, hr_r,
     ) = refs
     A0, SB0, R0 = ([[steps[(k * 3 + p) * 12 + i] for p in range(3)] for k in range(3)] for i in range(3))
     ACC, SB, RR = (
@@ -180,15 +180,27 @@
         res = dot(taps(ref, DIL[rate]), wd[rate, :, tap].reshape(3 * CH, BR))
         return to_tiles(res).reshape(16, OWN, 16, 128)
 
-    def whole(which, outer):
-        main = field(which, xpad)
-        if not outer:
-            return main
-        rim = field(which, hpad).reshape(16, OWN, 2, 8, 128)
-        last = rim[:, 0] + sum(
-            pltpu.roll(rim[:, j].reshape(32, 8, 128), 2 * j, 1).reshape(16, 2, 8, 128) for j in range(1, OWN)
-        )
-        return jnp.concatenate([main, last.reshape(16, 1, 16, 128)], axis=1)
+    hsent = []
+
+    def outer_send():
+        for f in range(4):
+            rim = field("point" if f == 3 else (f, 1), hpad).reshape(16, OWN, 2, 8, 128)
+            tile = rim[:, 0] + sum(
+                pltpu.roll(rim[:, j].reshape(32, 8, 128), 2 * j, 1).reshape(16, 2, 8, 128) for j in range(1, OWN)
+            )
+            tile = tile.reshape(16, 16, 128)
+            hb[:, f] = tile
+            hbs[:, f] = tile.astype(BF)
+        for m in range(1, 16):
+            hsent.append(send(hbs.at[beta_peer(m)], hr.at[m], hr_s.at[m], hr_r.at[m], chan_peer(m)))
+
+    def outer_end():
+        total = hb[beta]
+        for m in range(1, 16):
+            hsent[m - 1].wait_recv()
+            total = total + hr[m].astype(F32)
+        for f in range(4):
+            fin[f, OWN] = total[f]
 
     def compute(k):
         made = {}
@@ -196,7 +208,7 @@
             at = 0
             for which, lo, hi in CHUNKS[k][p]:
                 if which not in made:
-                    made[which] = whole(which, k == 2)
+                    made[which] = field(which, xpad)
                 t = made[which][:, lo:hi].reshape(2, 2, 2, 2, hi - lo, 16, 128)
                 A0[k][p][:, :, :, :, at : at + hi - lo] = t
                 SB0[k][p][:, :, :, :, at : at + hi - lo] = t.astype(BF)
@@ -244,7 +256,7 @@
                 if which == "point":
                     fin[3, lo:hi] = part
                 elif which[1] == 1:
-                    fin[which[0]] = part
+                    fin[which[0], :OWN] = part
                 else:
                     rate, tap = which
                     side, sign = (0, 1) if tap == 0 else (1, -1)
@@ -444,44 +456,46 @@
     pl.semaphore_wait(barrier, greeted)
     core_send(0)
     edge_start()
-    image_send()
-    tell_known()
     loads["wd0"].wait()
     compute(1)
     core_send(1)
+    image_send()
     halve(0, 0)
+    loads["wpt"].wait()
+    compute(2)
+    core_send(2)
+    halve(1, 0)
+    halve(2, 0)
     wt_step(0)
-    halve(1, 0)
-    loads["wpt"].wait()
+    tell_known()
     halve(0, 1)
     halve(1, 1)
+    halve(2, 1)
+    wt_step(1)
     edge_place()
-    compute(2)
-    core_send(2)
+    halve(0, 2)
+    halve(1, 2)
+    outer_send()
     image_near()
-    halve(0, 2)
-    halve(2, 0)
-    halve(1, 2)
-    wt_step(1)
+    halve(2, 2)
+    wt_step(2)
     finish(0)
     finish(1)
-    halve(2, 1)
+    finish(2)
+    merge_prepare()
+    wt_core()
+    outer_end()
     image_wide()
-    wt_step(2)
-    merge_prepare()
-    halve(2, 2)
-    wt_core()
     loads["bns"].wait()
     loads["bnt"].wait()
     loads["ms"].wait()
     loads["mt"].wait()
-    finish(2)
     for p in range(3):
         wsent[3, p].wait_recv()
     proj[...] = project(0, from_tiles(fin[3]))
+    proj[...] += branch_of(0)
+    proj[...] += branch_of(1)
     proj[...] += branch_of(2)
-    proj[...] += branch_of(1)
-    proj[...] += branch_of(0)
     gat[beta] = to_tiles(proj[...]).astype(BF)
     gsent = [send(gat.at[beta], gat.at[beta], ga_s.at[m], ga_r.at[m], chan_peer(m)) for m in range(1, 16)]
     offset = project(4, jnp.broadcast_to(image_end(), (32, BR)))[:8]
@@ -549,6 +563,7 @@
             dma((13,)), dma((3, 5)), dma((3, 3)), pltpu.SemaphoreType.REGULAR,
             dma((3, 4, 3)), dma((3, 4, 3)), dma((3, 2, 3)), dma((3, 2, 3)), dma((4, 3)), dma((4, 3)),
             dma((8,)), dma((8,)), dma((4,)), dma((4,)), dma((16,)), dma((16,)), dma((16,)), dma((16,)), dma((2,)), dma((2,)),
+            vm((16, 4, 16, 128), F32), vm((16, 4, 16, 128), BF), vm((16, 4, 16, 128), BF), dma((16,)), dma((16,)),
         ]
     )
     return pl.pallas_call(

time: 47.8 us -> 46.3 us (0.969)
  Pallas kernels: 46 us -> 44.5 us
    pallas_call x1, Pallas kernels: 46 us -> 44.5 us  [body(): pl.pallas_call(functools.partial(kernel, n_lon), out_shape=jax.ShapeDtype...]
where the time goes in v3:
time: 46.3 us; the launch traced here: 46.1 us
  Pallas kernels  44.5 us (96%)
  local copies, waits for them, and re-layouts  1.61 us (3%)
    pallas_call x1, Pallas kernels, body(): pl.pallas_call(functools.partial(kernel, n_lon), out_shape=jax.ShapeDtype...  44.5 us
    pallas_call x1, local copies, waits for them, and re-layouts, body(): pl.pallas_call(functools.partial(kernel, n_lon), out_shape=jax.ShapeDtype...  1.61 us

profile of v3, /device:TPU:1, one launch (start us, length us, event | category | flops | bytes accessed | tf_op | source)
XLA Modules:
  0.0 46.1 jit_solution(16324793955913670982)
XLA Ops:
  0.0 44.5 %aspp_head.1 = bf16[48,8,16]{2,1,0:T(8,128)(2,1)} custom-call(bf16[48,8,128]{2,1,0:T(8,128)(2,1)} %feat_h.1, bf16[128,256]{1,0:T(8,128)(2,1)} %wpt_h.1, bf16[3,3,3,128,256]{4,3,2,1,0:T(8,128)(2,1)} %wd_h.1, bf16[128,256]{1,0:T(8,128)(2,1)} %wpool_h.1, f32[5,256]{1,0:T(8,128)} %bns_h.1, f32[5,256]{1,0:T(8,128)} %bnt_h.1, bf16[5,16,256]{2,1,0:T(8,128)(2,1)} %bitcast.3, ...), custom_call_target="tpu_custom_call" | custom-call | tf_op jit(solution)/shard_map/aspp_head/pallas_call | solution.py:569
  44.5 1.6 %copy.14 = bf16[48,8,16]{0,2,1:T(8,128)(2,1)} copy(bf16[48,8,16]{2,1,0:T(8,128)(2,1)} %aspp_head.1) | data formatting | bytes 24576 | tf_op jit(solution)/shard_map/aspp_head/pallas_call | solution.py:569

commit v4 on v3

--- a/solution.py
+++ b/solution.py
@@ -73,7 +73,7 @@
     (
         fin, sh, rsh, wt0, wt1, wt2, ia, ib, ic, img, gat, wrow, wcat, vskip, vskip_out, proj,
         ld_sem, pw_sem, mw_sem, known,
-        rs_s, rs_r, sh_s, sh_r, wt_s, wt_r, ia_s, ia_r, ib_s, ib_r, ic_s, ic_r, ga_s, ga_r, ev_s, ev_r, hb, hbs, hr, hr_s, hr_r,
+        rs_s, rs_r, sh_s, sh_r, wt_s, wt_r, ia_s, ia_r, ib_s, ib_r, ic_s, ic_r, ga_s, ga_r, ev_s, ev_r, hb, hbs, hc, hq, hqs, hr, hr_s, hr_r,
     ) = refs
     A0, SB0, R0 = ([[steps[(k * 3 + p) * 12 + i] for p in range(3)] for k in range(3)] for i in range(3))
     ACC, SB, RR = (
@@ -191,13 +191,19 @@
             tile = tile.reshape(16, 16, 128)
             hb[:, f] = tile
             hbs[:, f] = tile.astype(BF)
-        for m in range(1, 16):
-            hsent.append(send(hbs.at[beta_peer(m)], hr.at[m], hr_s.at[m], hr_r.at[m], chan_peer(m)))
+        hsent.append(send(hbs.at[pl.ds((1 - c) * 8, 8)], hc, hr_s.at[8], hr_r.at[8], sibling))
+
+    def outer_chips():
+        hsent[0].wait_recv()
+        hq[...] = hb[pl.ds(c * 8, 8)] + hc[...].astype(F32)
+        hqs[...] = hq[...].astype(BF)
+        for m in range(1, 8):
+            hsent.append(send(hqs.at[beta_peer(m) - 8 * c], hr.at[m], hr_s.at[m], hr_r.at[m], chan_peer(m)))
 
     def outer_end():
-        total = hb[beta]
-        for m in range(1, 16):
-            hsent[m - 1].wait_recv()
+        total = hq[beta - 8 * c]
+        for m in range(1, 8):
+            hsent[m].wait_recv()
             total = total + hr[m].astype(F32)
         for f in range(4):
             fin[f, OWN] = total[f]
@@ -466,26 +472,27 @@
     core_send(2)
     halve(1, 0)
     halve(2, 0)
-    wt_step(0)
     tell_known()
     halve(0, 1)
     halve(1, 1)
+    wt_step(0)
     halve(2, 1)
-    wt_step(1)
     edge_place()
+    outer_send()
     halve(0, 2)
     halve(1, 2)
-    outer_send()
+    outer_chips()
     image_near()
+    wt_step(1)
     halve(2, 2)
-    wt_step(2)
     finish(0)
     finish(1)
     finish(2)
+    wt_step(2)
     merge_prepare()
+    image_wide()
     wt_core()
     outer_end()
-    image_wide()
     loads["bns"].wait()
     loads["bnt"].wait()
     loads["ms"].wait()
@@ -563,7 +570,8 @@
             dma((13,)), dma((3, 5)), dma((3, 3)), pltpu.SemaphoreType.REGULAR,
             dma((3, 4, 3)), dma((3, 4, 3)), dma((3, 2, 3)), dma((3, 2, 3)), dma((4, 3)), dma((4, 3)),
             dma((8,)), dma((8,)), dma((4,)), dma((4,)), dma((16,)), dma((16,)), dma((16,)), dma((16,)), dma((2,)), dma((2,)),
-            vm((16, 4, 16, 128), F32), vm((16, 4, 16, 128), BF), vm((16, 4, 16, 128), BF), dma((16,)), dma((16,)),
+            vm((16, 4, 16, 128), F32), vm((16, 4, 16, 128), BF), vm((8, 4, 16, 128), BF),
+            vm((8, 4, 16, 128), F32), vm((8, 4, 16, 128), BF), vm((8, 4, 16, 128), BF), dma((9,)), dma((9,)),
         ]
     )
     return pl.pallas_call(

time: 46.3 us -> 48.5 us (1.048)
  Pallas kernels: 44.5 us -> 46.7 us
    pallas_call x1, Pallas kernels: 44.5 us -> 46.7 us  [body(): pl.pallas_call(functools.partial(kernel, n_lon), out_shape=jax.ShapeDtype...]
where the time goes in v4:
time: 48.5 us; the launch traced here: 48.3 us
  Pallas kernels  46.7 us (96%)
  local copies, waits for them, and re-layouts  1.61 us (3%)
    pallas_call x1, Pallas kernels, body(): pl.pallas_call(functools.partial(kernel, n_lon), out_shape=jax.ShapeDtype...  46.7 us
    pallas_call x1, local copies, waits for them, and re-layouts, body(): pl.pallas_call(functools.partial(kernel, n_lon), out_shape=jax.ShapeDtype...  1.61 us

profile of v4, /device:TPU:1, one launch (start us, length us, event | category | flops | bytes accessed | tf_op | source)
XLA Modules:
  0.0 48.3 jit_solution(10948926549921159553)
XLA Ops:
  0.0 46.7 %aspp_head.1 = bf16[48,8,16]{2,1,0:T(8,128)(2,1)} custom-call(bf16[48,8,128]{2,1,0:T(8,128)(2,1)} %feat_h.1, bf16[128,256]{1,0:T(8,128)(2,1)} %wpt_h.1, bf16[3,3,3,128,256]{4,3,2,1,0:T(8,128)(2,1)} %wd_h.1, bf16[128,256]{1,0:T(8,128)(2,1)} %wpool_h.1, f32[5,256]{1,0:T(8,128)} %bns_h.1, f32[5,256]{1,0:T(8,128)} %bnt_h.1, bf16[5,16,256]{2,1,0:T(8,128)(2,1)} %bitcast.3, ...), custom_call_target="tpu_custom_call" | custom-call | tf_op jit(solution)/shard_map/aspp_head/pallas_call | solution.py:577
  46.7 1.6 %copy.14 = bf16[48,8,16]{0,2,1:T(8,128)(2,1)} copy(bf16[48,8,16]{2,1,0:T(8,128)(2,1)} %aspp_head.1) | data formatting | bytes 24576 | tf_op jit(solution)/shard_map/aspp_head/pallas_call | solution.py:577

commit v5 on v4

--- a/solution.py
+++ b/solution.py
@@ -472,27 +472,27 @@
     core_send(2)
     halve(1, 0)
     halve(2, 0)
+    wt_step(0)
     tell_known()
     halve(0, 1)
     halve(1, 1)
-    wt_step(0)
     halve(2, 1)
+    wt_step(1)
     edge_place()
     outer_send()
     halve(0, 2)
     halve(1, 2)
     outer_chips()
     image_near()
-    wt_step(1)
     halve(2, 2)
+    wt_step(2)
     finish(0)
     finish(1)
     finish(2)
-    wt_step(2)
     merge_prepare()
-    image_wide()
     wt_core()
     outer_end()
+    image_wide()
     loads["bns"].wait()
     loads["bnt"].wait()
     loads["ms"].wait()

time: 48.5 us -> 45.5 us (0.938)
  Pallas kernels: 46.7 us -> 43.7 us
    pallas_call x1, Pallas kernels: 46.7 us -> 43.7 us  [body(): pl.pallas_call(functools.partial(kernel, n_lon), out_shape=jax.ShapeDtype...]
where the time goes in v5:
time: 45.5 us; the launch traced here: 45.3 us
  Pallas kernels  43.7 us (96%)
  local copies, waits for them, and re-layouts  1.61 us (4%)
    pallas_call x1, Pallas kernels, body(): pl.pallas_call(functools.partial(kernel, n_lon), out_shape=jax.ShapeDtype...  43.7 us
    pallas_call x1, local copies, waits for them, and re-layouts, body(): pl.pallas_call(functools.partial(kernel, n_lon), out_shape=jax.ShapeDtype...  1.61 us

profile of v5, /device:TPU:1, one launch (start us, length us, event | category | flops | bytes accessed | tf_op | source)
XLA Modules:
  0.0 45.3 jit_solution(8664902174817066639)
XLA Ops:
  0.0 43.7 %aspp_head.1 = bf16[48,8,16]{2,1,0:T(8,128)(2,1)} custom-call(bf16[48,8,128]{2,1,0:T(8,128)(2,1)} %feat_h.1, bf16[128,256]{1,0:T(8,128)(2,1)} %wpt_h.1, bf16[3,3,3,128,256]{4,3,2,1,0:T(8,128)(2,1)} %wd_h.1, bf16[128,256]{1,0:T(8,128)(2,1)} %wpool_h.1, f32[5,256]{1,0:T(8,128)} %bns_h.1, f32[5,256]{1,0:T(8,128)} %bnt_h.1, bf16[5,16,256]{2,1,0:T(8,128)(2,1)} %bitcast.3, ...), custom_call_target="tpu_custom_call" | custom-call | tf_op jit(solution)/shard_map/aspp_head/pallas_call | solution.py:577
  43.7 1.6 %copy.14 = bf16[48,8,16]{0,2,1:T(8,128)(2,1)} copy(bf16[48,8,16]{2,1,0:T(8,128)(2,1)} %aspp_head.1) | data formatting | bytes 24576 | tf_op jit(solution)/shard_map/aspp_head/pallas_call | solution.py:577

commit v6 on v5

--- a/solution.py
+++ b/solution.py
@@ -28,6 +28,7 @@
 ORDERS = ((0, 2, 1), (2, 1, 0), (1, 0, 2))
 LANES = ((0, 512), (512, 896), (896, 1280))
 FAR = {(0, 0): (2, 1), (0, 2): (1, 2), (1, 0): (3, 4, 2), (1, 2): (3, 2, 4), (2, 0): (5, 4), (2, 2): (4, 5)}
+FARTHEST = (7, 15, 5, 6, 13, 14, 3, 11, 4, 12, 1, 2, 9, 10, 8)
 GRAY = ((0, 0), (0, 1), (1, 1), (1, 0))
 
 
@@ -97,8 +98,53 @@
         ]
     ):
         loads[name] = pltpu.make_async_copy(src, dst, ld_sem.at[i])
+        if i < 3:
+            loads[name].start()
+
+    def chan_peer(m):
+        mc, mx, mh, ml = (m >> 3) & 1, (m >> 2) & 1, (m >> 1) & 1, m & 1
+        pc = 1 - c if mc else c
+        pa = 1 - a if mx else a
+        flip = y + 1 - 2 * (y % 2)
+        py = {(0, 0): y, (0, 1): flip, (1, 0): 3 - y, (1, 1): (y + 2) % 4}[(mh, ml)]
+        return (lon, pa * 8 + py * 2 + pc)
+
+    def beta_peer(m):
+        bits = [c, *bit]
+        masks = [(m >> 3) & 1, (m >> 2) & 1, (m >> 1) & 1, m & 1]
+        f = [1 - b if k else b for b, k in zip(bits, masks)]
+        return f[0] * 8 + f[1] * 4 + f[2] * 2 + f[3]
+
+    sibling = chan_peer(8)
+    step_peer = (chan_peer(4), chan_peer(2), chan_peer(1))
+
+    def lon_peer(k):
+        return ((lon + k + n_lon) % n_lon, chan)
+
+    def lon_xor(m):
+        out = lon
+        for p in range(5):
+            if (m >> p) & 1:
+                b = (lon // (1 << p)) % 2
+                out = out + (1 - 2 * b) * (1 << p)
+        return (out, chan)
+
+    near = list(range(1, 8))
+    blocks = n_lon // 8
+
+    barrier = pltpu.get_barrier_semaphore()
+    greeted = 0
+    for dev in (
+        ([lon_peer(8), lon_peer(-8)] if blocks > 1 else [])
+        + [lon_peer(k) for k in (5, -5, 4, -4, 3, -3, 2, -2, 1, -1)]
+        + [lon_xor(m) for m in near]
+        + [chan_peer(m) for m in range(1, 16)]
+    ):
+        pl.semaphore_signal(barrier, inc=1, device_id=dev, device_id_type=MESH)
+        greeted += 1
+
+    for name in list(loads)[3:]:
         loads[name].start()
-
     for p, ((s, e), ref) in enumerate(zip(LANES, (wt0, wt1, wt2))):
         loads[f"wt{p}"] = Several()
         for b in range(5):
@@ -117,48 +163,6 @@
             cp = pltpu.make_async_copy(mw_h.at[t, b], wrow.at[t, 16 * b : 16 * b + 16], mw_sem.at[t, b])
             cp.start()
             loads["mw"].copies.append(cp)
-
-    def chan_peer(m):
-        mc, mx, mh, ml = (m >> 3) & 1, (m >> 2) & 1, (m >> 1) & 1, m & 1
-        pc = 1 - c if mc else c
-        pa = 1 - a if mx else a
-        flip = y + 1 - 2 * (y % 2)
-        py = {(0, 0): y, (0, 1): flip, (1, 0): 3 - y, (1, 1): (y + 2) % 4}[(mh, ml)]
-        return (lon, pa * 8 + py * 2 + pc)
-
-    def beta_peer(m):
-        bits = [c, *bit]
-        masks = [(m >> 3) & 1, (m >> 2) & 1, (m >> 1) & 1, m & 1]
-        f = [1 - b if k else b for b, k in zip(bits, masks)]
-        return f[0] * 8 + f[1] * 4 + f[2] * 2 + f[3]
-
-    sibling = chan_peer(8)
-    step_peer = (chan_peer(4), chan_peer(2), chan_peer(1))
-
-    def lon_peer(k):
-        return ((lon + k + n_lon) % n_lon, chan)
-
-    def lon_xor(m):
-        out = lon
-        for p in range(5):
-            if (m >> p) & 1:
-                b = (lon // (1 << p)) % 2
-                out = out + (1 - 2 * b) * (1 << p)
-        return (out, chan)
-
-    near = list(range(1, 8))
-    blocks = n_lon // 8
-
-    barrier = pltpu.get_barrier_semaphore()
-    greeted = 0
-    for dev in (
-        [chan_peer(m) for m in range(1, 16)]
-        + [lon_peer(k) for k in (1, 2, 3, 4, 5, -1, -2, -3, -4, -5)]
-        + [lon_xor(m) for m in near]
-        + ([lon_peer(8), lon_peer(-8)] if blocks > 1 else [])
-    ):
-        pl.semaphore_signal(barrier, inc=1, device_id=dev, device_id_type=MESH)
-        greeted += 1
 
     sends = []
 
@@ -504,7 +508,7 @@
     proj[...] += branch_of(1)
     proj[...] += branch_of(2)
     gat[beta] = to_tiles(proj[...]).astype(BF)
-    gsent = [send(gat.at[beta], gat.at[beta], ga_s.at[m], ga_r.at[m], chan_peer(m)) for m in range(1, 16)]
+    gsent = [send(gat.at[beta], gat.at[beta], ga_s.at[m], ga_r.at[m], chan_peer(m)) for m in FARTHEST]
     offset = project(4, jnp.broadcast_to(image_end(), (32, BR)))[:8]
     for g in gsent:
         g.wait_recv()

time: 45.5 us -> 45 us (0.989)
  Pallas kernels: 43.7 us -> 43.2 us
    pallas_call x1, Pallas kernels: 43.7 us -> 43.2 us  [body(): pl.pallas_call(functools.partial(kernel, n_lon), out_shape=jax.ShapeDtype...]
where the time goes in v6:
time: 45 us; the launch traced here: 44.8 us
  Pallas kernels  43.2 us (96%)
  local copies, waits for them, and re-layouts  1.61 us (4%)
    pallas_call x1, Pallas kernels, body(): pl.pallas_call(functools.partial(kernel, n_lon), out_shape=jax.ShapeDtype...  43.2 us
    pallas_call x1, local copies, waits for them, and re-layouts, body(): pl.pallas_call(functools.partial(kernel, n_lon), out_shape=jax.ShapeDtype...  1.61 us

profile of v6, /device:TPU:1, one launch (start us, length us, event | category | flops | bytes accessed | tf_op | source)
XLA Modules:
  0.0 44.8 jit_solution(13272878735037822727)
XLA Ops:
  0.0 43.2 %aspp_head.1 = bf16[48,8,16]{2,1,0:T(8,128)(2,1)} custom-call(bf16[48,8,128]{2,1,0:T(8,128)(2,1)} %feat_h.1, bf16[128,256]{1,0:T(8,128)(2,1)} %wpt_h.1, bf16[3,3,3,128,256]{4,3,2,1,0:T(8,128)(2,1)} %wd_h.1, bf16[128,256]{1,0:T(8,128)(2,1)} %wpool_h.1, f32[5,256]{1,0:T(8,128)} %bns_h.1, f32[5,256]{1,0:T(8,128)} %bnt_h.1, bf16[5,16,256]{2,1,0:T(8,128)(2,1)} %bitcast.3, ...), custom_call_target="tpu_custom_call" | custom-call | tf_op jit(solution)/shard_map/aspp_head/pallas_call | solution.py:581
  43.2 1.6 %copy.14 = bf16[48,8,16]{0,2,1:T(8,128)(2,1)} copy(bf16[48,8,16]{2,1,0:T(8,128)(2,1)} %aspp_head.1) | data formatting | bytes 24576 | tf_op jit(solution)/shard_map/aspp_head/pallas_call | solution.py:581
